TPU v7x, 512 devices: a whole 4x8x8 slice. The times are simulated.
512 devices in a mesh: wide: 32 (over z_hi, y, core), narrow: 16 (over x, z_lo).
Axes of the slice: x: 4, y: 8, z: 8 (z_hi: 2, z_lo: 4; z = z_hi * 4 + z_lo), core: 2. Of those that a mesh axis runs over, the one named last changes fastest.
Arguments:
- image_embed: bfloat16 [8192, 1152], P(('wide', 'narrow')), may hold values from -0.59765625 to 0.59765625
- text_embed: bfloat16 [8192, 1152], P(('wide', 'narrow')), may hold values from -0.59765625 to 0.59765625
- logit_scale: float32 [1], replicated, may hold values from 2 to 8
- logit_bias: float32 [1], replicated, may hold values from -8 to -4
Outputs:
- loss: float32 [1], replicated
- image_grad: float32 [8192, 1152], P(('wide', 'narrow'))
- text_grad: float32 [8192, 1152], P(('wide', 'narrow'))
All inputs are finite; a program needn't handle non-finite values.
Results may differ from a plain program's by a relative error of at most 0.0025.
Values may be sent and summed in bfloat16 or wider, within the bound.
A program may use at most 64 MiB of HBM per device.

v0:
```python
import jax
import jax.numpy as jnp
from jax import lax
from jax.sharding import PartitionSpec as P


def from_behind(x, axis, by):
    length = lax.axis_size(axis)
    return lax.ppermute(x, axis, [(i, (i + by) % length) for i in range(length)])


def pair_terms(images, text_block, image_rows, text_rows, scaling, offset):
    logits = (
        scaling
        * lax.dot_general(
            images, text_block, (((1,), (1,)), ((), ())), preferred_element_type=jnp.float32
        )
        + offset
    )
    label_sign = jnp.where(image_rows[:, None] == text_rows[None, :], 1.0, -1.0).astype(jnp.float32)
    signed = label_sign * logits
    loss_part = jnp.sum(jax.nn.softplus(-signed))
    weights = (scaling * (-label_sign * jax.nn.sigmoid(-signed))).astype(jnp.bfloat16)
    grad_text = lax.dot_general(
        weights, images, (((0,), (0,)), ((), ())), preferred_element_type=jnp.float32
    )
    return (loss_part, weights, grad_text)


def local(image_embed, text_embed, logit_scale, logit_bias):
    row_count = text_embed.shape[0]
    feature_count = text_embed.shape[1]
    wide_count = lax.axis_size("wide")
    wide_place = lax.axis_index("wide")
    narrow_place = lax.axis_index("narrow")
    scaling = logit_scale[0]
    offset = logit_bias[0]
    images = lax.all_gather(image_embed, "narrow", axis=0, tiled=True)
    group_rows = images.shape[0]
    image_rows = wide_place * group_rows + jnp.arange(group_rows, dtype=jnp.int32)

    def visit(text_block, anchor):
        text_rows = (
            anchor * group_rows
            + narrow_place * row_count
            + jnp.arange(text_block.shape[0], dtype=jnp.int32)
        )
        return pair_terms(images, text_block, image_rows, text_rows, scaling, offset)

    loss_zero = jnp.zeros((), jnp.float32)
    hops = jnp.arange(wide_count, dtype=jnp.int32)

    def advance(state, hop):
        text_block, grad_accum, loss_sum = state
        loss_one, weights_one, grad_one = visit(text_block, (wide_place - hop) % wide_count)
        grad_accum = grad_accum + grad_one
        outputs = (weights_one, text_block)
        text_block = from_behind(text_block, "wide", 1)
        grad_accum = from_behind(grad_accum, "wide", 1)
        return ((text_block, grad_accum, loss_sum + loss_one), outputs)

    start_state = (text_embed, jnp.zeros((row_count, feature_count), jnp.float32), loss_zero)
    final_state, stacks = lax.scan(advance, start_state, hops)
    text_grad = final_state[1]
    loss_sum = final_state[2]
    weight_stack, text_stack = stacks
    image_terms = jnp.einsum(
        "sgr,srd->gd", weight_stack, text_stack, preferred_element_type=jnp.float32
    )
    image_grad = lax.psum_scatter(image_terms, "narrow", scatter_dimension=0, tiled=True)
    loss_all = lax.psum(loss_sum, ("wide", "narrow"))
    loss = (loss_all / (group_rows * wide_count)).reshape(1)
    return (loss, image_grad, text_grad)


def solution(mesh):
    in_specs = (P(("wide", "narrow"), None), P(("wide", "narrow"), None), P(), P())
    out_specs = (P(), P(("wide", "narrow"), None), P(("wide", "narrow"), None))
    return jax.shard_map(local, mesh=mesh, in_specs=in_specs, out_specs=out_specs, check_vma=False)
```

profile of v0, /device:TPU:1, one launch (start us, length us, event | category | flops | bytes accessed | tf_op | source)
XLA Modules:
  0.0 754.5 jit_solution(13964787738829796925)
XLA Ops:
  8.0 44.2 %all_gather.3 = bf16[256,1152]{1,0:T(8,128)(2,1)S(1)} all-gather(bf16[16,1152]{1,0:T(8,128)(2,1)} %param.6), channel_id=1, replica_groups=mesh['wide'=32,'narrow'=16] {'narrow'}, dimensions={0}, use_global_device_ids=true | all-gather | bytes 626688 | tf_op jit(solution)/shard_map/all_gather | solution.py:38
  52.2 584.1 %while.21 = (s32[]{:T(128)}, bf16[16,1152]{1,0:T(8,128)(2,1)S(1)}, f32[16,1152]{1,0:T(8,128)S(1)}, f32[]{:T(128)}, bf16[32,256,16]{1,2,0:T(8,128)(2,1)S(1)}, /*i...) while((s32[]{:T(128)}, bf16[16,1152]{1,0:T(8,128)(2,1)S(1)}, ...), condition=%wide.region_2.3_spmd.clone, body=%wide.region_0.2_spmd.clone.sunk | while | flops 19011872 | bytes 2016386 | solution.py:63
  52.3 11.0 %collective-permute-start = (bf16[16,1152]{1,0:T(8,128)(2,1)S(1)}, bf16[16,1152]{1,0:T(8,128)(2,1)S(1)}, u32[]{:S(2)}, u32[]{:S(2)}) collective-permute-start(bf16[16,1152]{1,0:T(8,128)(2,1)S(1)} %copy.20), channel_id=1, source_target_pairs={{0,16},{16,32},{32,48},{48,64},{64,80},{80,96},{96,112},{112,128},... | collective-permute-start | bytes 110600 | tf_op jit(solution)/shard_map/while/body/eval_jaxpr/ppermute | solution.py:9
  64.6 2.2 fusion.23
  71.1 4.2 collective-permute-start
  76.6 2.2 fusion.23
  83.0 4.9 collective-permute-done.1
  91.1 2.2 fusion.23
  97.6 2.5 collective-permute-done
  100.0 6.4 collective-permute-done.1
  109.6 2.2 fusion.23
  116.1 2.5 collective-permute-done
  118.5 6.4 collective-permute-done.1
  128.1 2.2 fusion.23
  134.6 2.5 collective-permute-done
  137.0 6.4 collective-permute-done.1
  153.1 2.5 collective-permute-done
  155.5 6.4 collective-permute-done.1
  171.6 2.5 collective-permute-done
  174.1 6.4 collective-permute-done.1
  183.7 2.2 fusion.23
  190.1 2.5 collective-permute-done
  192.6 6.4 collective-permute-done.1
  208.6 2.5 collective-permute-done
  211.1 6.4 collective-permute-done.1
  220.7 2.2 fusion.23
  227.1 2.5 collective-permute-done
  229.6 6.4 collective-permute-done.1
  245.6 2.5 collective-permute-done
  248.1 6.4 collective-permute-done.1
  264.1 2.4 collective-permute-done
  266.5 6.4 collective-permute-done.1
  282.5 2.4 collective-permute-done
  284.9 6.4 collective-permute-done.1
  301.0 2.3 collective-permute-done
  303.3 6.4 collective-permute-done.1
  321.5 6.4 collective-permute-done.1
  331.1 2.2 fusion.23
  339.5 6.4 collective-permute-done.1
  357.5 6.4 collective-permute-done.1
  367.1 2.2 fusion.23
  375.5 6.4 collective-permute-done.1
  393.5 6.4 collective-permute-done.1
  411.5 6.4 collective-permute-done.1
  429.6 6.4 collective-permute-done.1
  447.6 6.4 collective-permute-done.1
  465.6 6.4 collective-permute-done.1
  483.6 6.4 collective-permute-done.1
  501.6 6.4 collective-permute-done.1
  519.6 6.4 collective-permute-done.1
  535.7 2.3 collective-permute-done
  538.0 6.4 collective-permute-done.1
  554.0 2.4 collective-permute-done
  556.4 6.4 collective-permute-done.1
  566.0 2.2 fusion.23
  572.4 2.4 collective-permute-done
  574.8 6.4 collective-permute-done.1
  590.9 2.4 collective-permute-done
  593.2 6.4 collective-permute-done.1
  609.3 2.4 collective-permute-done
  611.6 6.4 collective-permute-done.1
  627.7 2.3 collective-permute-done
  630.0 6.4 collective-permute-done.1
  637.9 107.3 %psum.7 = f32[]{:T(128)} all-reduce(f32[]{:T(128)} %get-tuple-element.170), channel_id=1, replica_groups=mesh['wide'=32,'narrow'=16] {'wide','narrow'}, use_global_device_ids=true, to_apply=%region_3.4 | all-reduce | flops 1 | bytes 8 | tf_op jit(solution)/shard_map/psum | solution.py:71
  (333 shorter events, 266.5 us)
Async XLA Ops:
  7.2 738.7 %reduce-scatter.2.cloned.1.call-start = ((), (), s32[]{:S(2)}) async-start(), calls=%async_computation.1 | async-start | bytes 1253376 | tf_op jit(solution)/shard_map/reduce_scatter | solution.py:70
  52.3 18.8 %collective-permute-start = (bf16[16,1152]{1,0:T(8,128)(2,1)S(1)}, bf16[16,1152]{1,0:T(8,128)(2,1)S(1)}, u32[]{:S(2)}, u32[]{:S(2)}) collective-permute-start(bf16[16,1152]{1,0:T(8,128)(2,1)S(1)} %copy.20), channel_id=1, source_target_pairs={{0,16},{16,32},{32,48},{48,64},{64,80},{80,96},{96,112},{112,128},... | collective-permute-start | bytes 110600 | tf_op jit(solution)/shard_map/while/body/eval_jaxpr/ppermute | solution.py:9
  71.1 12.0 %collective-permute-start = (bf16[16,1152]{1,0:T(8,128)(2,1)S(1)}, bf16[16,1152]{1,0:T(8,128)(2,1)S(1)}, u32[]{:S(2)}, u32[]{:S(2)}) collective-permute-start(bf16[16,1152]{1,0:T(8,128)(2,1)S(1)} %copy.20), channel_id=1, source_target_pairs={{0,16},{16,32},{32,48},{48,64},{64,80},{80,96},{96,112},{112,128},... | collective-permute-start | bytes 110600 | tf_op jit(solution)/shard_map/while/body/eval_jaxpr/ppermute | solution.py:9
  79.7 8.2 %collective-permute-start.1 = (f32[16,1152]{1,0:T(8,128)S(1)}, f32[16,1152]{1,0:T(8,128)S(1)}, u32[]{:S(2)}, u32[]{:S(2)}) collective-permute-start(f32[16,1152]{1,0:T(8,128)S(1)} %convolution_add_fusion.2), channel_id=1, source_target_pairs={{0,16},{16,32},{32,48},{48,64},{64,80},{80,96},{96,112},{112,128},... | collective-permute-start | bytes 221192 | tf_op jit(solution)/shard_map/while/body/eval_jaxpr/ppermute | solution.py:9
  87.9 12.1 %collective-permute-start = (bf16[16,1152]{1,0:T(8,128)(2,1)S(1)}, bf16[16,1152]{1,0:T(8,128)(2,1)S(1)}, u32[]{:S(2)}, u32[]{:S(2)}) collective-permute-start(bf16[16,1152]{1,0:T(8,128)(2,1)S(1)} %copy.20), channel_id=1, source_target_pairs={{0,16},{16,32},{32,48},{48,64},{64,80},{80,96},{96,112},{112,128},... | collective-permute-start | bytes 110600 | tf_op jit(solution)/shard_map/while/body/eval_jaxpr/ppermute | solution.py:9
  94.2 12.2 %collective-permute-start.1 = (f32[16,1152]{1,0:T(8,128)S(1)}, f32[16,1152]{1,0:T(8,128)S(1)}, u32[]{:S(2)}, u32[]{:S(2)}) collective-permute-start(f32[16,1152]{1,0:T(8,128)S(1)} %convolution_add_fusion.2), channel_id=1, source_target_pairs={{0,16},{16,32},{32,48},{48,64},{64,80},{80,96},{96,112},{112,128},... | collective-permute-start | bytes 221192 | tf_op jit(solution)/shard_map/while/body/eval_jaxpr/ppermute | solution.py:9
  106.4 12.1 %collective-permute-start = (bf16[16,1152]{1,0:T(8,128)(2,1)S(1)}, bf16[16,1152]{1,0:T(8,128)(2,1)S(1)}, u32[]{:S(2)}, u32[]{:S(2)}) collective-permute-start(bf16[16,1152]{1,0:T(8,128)(2,1)S(1)} %copy.20), channel_id=1, source_target_pairs={{0,16},{16,32},{32,48},{48,64},{64,80},{80,96},{96,112},{112,128},... | collective-permute-start | bytes 110600 | tf_op jit(solution)/shard_map/while/body/eval_jaxpr/ppermute | solution.py:9
  112.7 12.2 %collective-permute-start.1 = (f32[16,1152]{1,0:T(8,128)S(1)}, f32[16,1152]{1,0:T(8,128)S(1)}, u32[]{:S(2)}, u32[]{:S(2)}) collective-permute-start(f32[16,1152]{1,0:T(8,128)S(1)} %convolution_add_fusion.2), channel_id=1, source_target_pairs={{0,16},{16,32},{32,48},{48,64},{64,80},{80,96},{96,112},{112,128},... | collective-permute-start | bytes 221192 | tf_op jit(solution)/shard_map/while/body/eval_jaxpr/ppermute | solution.py:9
  124.9 12.1 %collective-permute-start = (bf16[16,1152]{1,0:T(8,128)(2,1)S(1)}, bf16[16,1152]{1,0:T(8,128)(2,1)S(1)}, u32[]{:S(2)}, u32[]{:S(2)}) collective-permute-start(bf16[16,1152]{1,0:T(8,128)(2,1)S(1)} %copy.20), channel_id=1, source_target_pairs={{0,16},{16,32},{32,48},{48,64},{64,80},{80,96},{96,112},{112,128},... | collective-permute-start | bytes 110600 | tf_op jit(solution)/shard_map/while/body/eval_jaxpr/ppermute | solution.py:9
  131.2 12.2 %collective-permute-start.1 = (f32[16,1152]{1,0:T(8,128)S(1)}, f32[16,1152]{1,0:T(8,128)S(1)}, u32[]{:S(2)}, u32[]{:S(2)}) collective-permute-start(f32[16,1152]{1,0:T(8,128)S(1)} %convolution_add_fusion.2), channel_id=1, source_target_pairs={{0,16},{16,32},{32,48},{48,64},{64,80},{80,96},{96,112},{112,128},... | collective-permute-start | bytes 221192 | tf_op jit(solution)/shard_map/while/body/eval_jaxpr/ppermute | solution.py:9
  143.4 12.1 %collective-permute-start = (bf16[16,1152]{1,0:T(8,128)(2,1)S(1)}, bf16[16,1152]{1,0:T(8,128)(2,1)S(1)}, u32[]{:S(2)}, u32[]{:S(2)}) collective-permute-start(bf16[16,1152]{1,0:T(8,128)(2,1)S(1)} %copy.20), channel_id=1, source_target_pairs={{0,16},{16,32},{32,48},{48,64},{64,80},{80,96},{96,112},{112,128},... | collective-permute-start | bytes 110600 | tf_op jit(solution)/shard_map/while/body/eval_jaxpr/ppermute | solution.py:9
  149.8 12.2 %collective-permute-start.1 = (f32[16,1152]{1,0:T(8,128)S(1)}, f32[16,1152]{1,0:T(8,128)S(1)}, u32[]{:S(2)}, u32[]{:S(2)}) collective-permute-start(f32[16,1152]{1,0:T(8,128)S(1)} %convolution_add_fusion.2), channel_id=1, source_target_pairs={{0,16},{16,32},{32,48},{48,64},{64,80},{80,96},{96,112},{112,128},... | collective-permute-start | bytes 221192 | tf_op jit(solution)/shard_map/while/body/eval_jaxpr/ppermute | solution.py:9
  161.9 12.1 %collective-permute-start = (bf16[16,1152]{1,0:T(8,128)(2,1)S(1)}, bf16[16,1152]{1,0:T(8,128)(2,1)S(1)}, u32[]{:S(2)}, u32[]{:S(2)}) collective-permute-start(bf16[16,1152]{1,0:T(8,128)(2,1)S(1)} %copy.20), channel_id=1, source_target_pairs={{0,16},{16,32},{32,48},{48,64},{64,80},{80,96},{96,112},{112,128},... | collective-permute-start | bytes 110600 | tf_op jit(solution)/shard_map/while/body/eval_jaxpr/ppermute | solution.py:9
  168.3 12.2 %collective-permute-start.1 = (f32[16,1152]{1,0:T(8,128)S(1)}, f32[16,1152]{1,0:T(8,128)S(1)}, u32[]{:S(2)}, u32[]{:S(2)}) collective-permute-start(f32[16,1152]{1,0:T(8,128)S(1)} %convolution_add_fusion.2), channel_id=1, source_target_pairs={{0,16},{16,32},{32,48},{48,64},{64,80},{80,96},{96,112},{112,128},... | collective-permute-start | bytes 221192 | tf_op jit(solution)/shard_map/while/body/eval_jaxpr/ppermute | solution.py:9
  180.4 12.1 %collective-permute-start = (bf16[16,1152]{1,0:T(8,128)(2,1)S(1)}, bf16[16,1152]{1,0:T(8,128)(2,1)S(1)}, u32[]{:S(2)}, u32[]{:S(2)}) collective-permute-start(bf16[16,1152]{1,0:T(8,128)(2,1)S(1)} %copy.20), channel_id=1, source_target_pairs={{0,16},{16,32},{32,48},{48,64},{64,80},{80,96},{96,112},{112,128},... | collective-permute-start | bytes 110600 | tf_op jit(solution)/shard_map/while/body/eval_jaxpr/ppermute | solution.py:9
  186.8 12.2 %collective-permute-start.1 = (f32[16,1152]{1,0:T(8,128)S(1)}, f32[16,1152]{1,0:T(8,128)S(1)}, u32[]{:S(2)}, u32[]{:S(2)}) collective-permute-start(f32[16,1152]{1,0:T(8,128)S(1)} %convolution_add_fusion.2), channel_id=1, source_target_pairs={{0,16},{16,32},{32,48},{48,64},{64,80},{80,96},{96,112},{112,128},... | collective-permute-start | bytes 221192 | tf_op jit(solution)/shard_map/while/body/eval_jaxpr/ppermute | solution.py:9
  198.9 12.1 %collective-permute-start = (bf16[16,1152]{1,0:T(8,128)(2,1)S(1)}, bf16[16,1152]{1,0:T(8,128)(2,1)S(1)}, u32[]{:S(2)}, u32[]{:S(2)}) collective-permute-start(bf16[16,1152]{1,0:T(8,128)(2,1)S(1)} %copy.20), channel_id=1, source_target_pairs={{0,16},{16,32},{32,48},{48,64},{64,80},{80,96},{96,112},{112,128},... | collective-permute-start | bytes 110600 | tf_op jit(solution)/shard_map/while/body/eval_jaxpr/ppermute | solution.py:9
  205.3 12.2 %collective-permute-start.1 = (f32[16,1152]{1,0:T(8,128)S(1)}, f32[16,1152]{1,0:T(8,128)S(1)}, u32[]{:S(2)}, u32[]{:S(2)}) collective-permute-start(f32[16,1152]{1,0:T(8,128)S(1)} %convolution_add_fusion.2), channel_id=1, source_target_pairs={{0,16},{16,32},{32,48},{48,64},{64,80},{80,96},{96,112},{112,128},... | collective-permute-start | bytes 221192 | tf_op jit(solution)/shard_map/while/body/eval_jaxpr/ppermute | solution.py:9
  217.4 12.1 %collective-permute-start = (bf16[16,1152]{1,0:T(8,128)(2,1)S(1)}, bf16[16,1152]{1,0:T(8,128)(2,1)S(1)}, u32[]{:S(2)}, u32[]{:S(2)}) collective-permute-start(bf16[16,1152]{1,0:T(8,128)(2,1)S(1)} %copy.20), channel_id=1, source_target_pairs={{0,16},{16,32},{32,48},{48,64},{64,80},{80,96},{96,112},{112,128},... | collective-permute-start | bytes 110600 | tf_op jit(solution)/shard_map/while/body/eval_jaxpr/ppermute | solution.py:9
  223.8 12.2 %collective-permute-start.1 = (f32[16,1152]{1,0:T(8,128)S(1)}, f32[16,1152]{1,0:T(8,128)S(1)}, u32[]{:S(2)}, u32[]{:S(2)}) collective-permute-start(f32[16,1152]{1,0:T(8,128)S(1)} %convolution_add_fusion.2), channel_id=1, source_target_pairs={{0,16},{16,32},{32,48},{48,64},{64,80},{80,96},{96,112},{112,128},... | collective-permute-start | bytes 221192 | tf_op jit(solution)/shard_map/while/body/eval_jaxpr/ppermute | solution.py:9
  236.0 12.1 %collective-permute-start = (bf16[16,1152]{1,0:T(8,128)(2,1)S(1)}, bf16[16,1152]{1,0:T(8,128)(2,1)S(1)}, u32[]{:S(2)}, u32[]{:S(2)}) collective-permute-start(bf16[16,1152]{1,0:T(8,128)(2,1)S(1)} %copy.20), channel_id=1, source_target_pairs={{0,16},{16,32},{32,48},{48,64},{64,80},{80,96},{96,112},{112,128},... | collective-permute-start | bytes 110600 | tf_op jit(solution)/shard_map/while/body/eval_jaxpr/ppermute | solution.py:9
  242.3 12.2 %collective-permute-start.1 = (f32[16,1152]{1,0:T(8,128)S(1)}, f32[16,1152]{1,0:T(8,128)S(1)}, u32[]{:S(2)}, u32[]{:S(2)}) collective-permute-start(f32[16,1152]{1,0:T(8,128)S(1)} %convolution_add_fusion.2), channel_id=1, source_target_pairs={{0,16},{16,32},{32,48},{48,64},{64,80},{80,96},{96,112},{112,128},... | collective-permute-start | bytes 221192 | tf_op jit(solution)/shard_map/while/body/eval_jaxpr/ppermute | solution.py:9
  254.5 12.1 %collective-permute-start = (bf16[16,1152]{1,0:T(8,128)(2,1)S(1)}, bf16[16,1152]{1,0:T(8,128)(2,1)S(1)}, u32[]{:S(2)}, u32[]{:S(2)}) collective-permute-start(bf16[16,1152]{1,0:T(8,128)(2,1)S(1)} %copy.20), channel_id=1, source_target_pairs={{0,16},{16,32},{32,48},{48,64},{64,80},{80,96},{96,112},{112,128},... | collective-permute-start | bytes 110600 | tf_op jit(solution)/shard_map/while/body/eval_jaxpr/ppermute | solution.py:9
  260.8 12.1 %collective-permute-start.1 = (f32[16,1152]{1,0:T(8,128)S(1)}, f32[16,1152]{1,0:T(8,128)S(1)}, u32[]{:S(2)}, u32[]{:S(2)}) collective-permute-start(f32[16,1152]{1,0:T(8,128)S(1)} %convolution_add_fusion.2), channel_id=1, source_target_pairs={{0,16},{16,32},{32,48},{48,64},{64,80},{80,96},{96,112},{112,128},... | collective-permute-start | bytes 221192 | tf_op jit(solution)/shard_map/while/body/eval_jaxpr/ppermute | solution.py:9
  272.9 12.0 %collective-permute-start = (bf16[16,1152]{1,0:T(8,128)(2,1)S(1)}, bf16[16,1152]{1,0:T(8,128)(2,1)S(1)}, u32[]{:S(2)}, u32[]{:S(2)}) collective-permute-start(bf16[16,1152]{1,0:T(8,128)(2,1)S(1)} %copy.20), channel_id=1, source_target_pairs={{0,16},{16,32},{32,48},{48,64},{64,80},{80,96},{96,112},{112,128},... | collective-permute-start | bytes 110600 | tf_op jit(solution)/shard_map/while/body/eval_jaxpr/ppermute | solution.py:9
  279.2 12.1 %collective-permute-start.1 = (f32[16,1152]{1,0:T(8,128)S(1)}, f32[16,1152]{1,0:T(8,128)S(1)}, u32[]{:S(2)}, u32[]{:S(2)}) collective-permute-start(f32[16,1152]{1,0:T(8,128)S(1)} %convolution_add_fusion.2), channel_id=1, source_target_pairs={{0,16},{16,32},{32,48},{48,64},{64,80},{80,96},{96,112},{112,128},... | collective-permute-start | bytes 221192 | tf_op jit(solution)/shard_map/while/body/eval_jaxpr/ppermute | solution.py:9
  291.3 11.9 %collective-permute-start = (bf16[16,1152]{1,0:T(8,128)(2,1)S(1)}, bf16[16,1152]{1,0:T(8,128)(2,1)S(1)}, u32[]{:S(2)}, u32[]{:S(2)}) collective-permute-start(bf16[16,1152]{1,0:T(8,128)(2,1)S(1)} %copy.20), channel_id=1, source_target_pairs={{0,16},{16,32},{32,48},{48,64},{64,80},{80,96},{96,112},{112,128},... | collective-permute-start | bytes 110600 | tf_op jit(solution)/shard_map/while/body/eval_jaxpr/ppermute | solution.py:9
  297.6 12.0 %collective-permute-start.1 = (f32[16,1152]{1,0:T(8,128)S(1)}, f32[16,1152]{1,0:T(8,128)S(1)}, u32[]{:S(2)}, u32[]{:S(2)}) collective-permute-start(f32[16,1152]{1,0:T(8,128)S(1)} %convolution_add_fusion.2), channel_id=1, source_target_pairs={{0,16},{16,32},{32,48},{48,64},{64,80},{80,96},{96,112},{112,128},... | collective-permute-start | bytes 221192 | tf_op jit(solution)/shard_map/while/body/eval_jaxpr/ppermute | solution.py:9
  309.7 11.8 %collective-permute-start = (bf16[16,1152]{1,0:T(8,128)(2,1)S(1)}, bf16[16,1152]{1,0:T(8,128)(2,1)S(1)}, u32[]{:S(2)}, u32[]{:S(2)}) collective-permute-start(bf16[16,1152]{1,0:T(8,128)(2,1)S(1)} %copy.20), channel_id=1, source_target_pairs={{0,16},{16,32},{32,48},{48,64},{64,80},{80,96},{96,112},{112,128},... | collective-permute-start | bytes 110600 | tf_op jit(solution)/shard_map/while/body/eval_jaxpr/ppermute | solution.py:9
  316.0 11.9 %collective-permute-start.1 = (f32[16,1152]{1,0:T(8,128)S(1)}, f32[16,1152]{1,0:T(8,128)S(1)}, u32[]{:S(2)}, u32[]{:S(2)}) collective-permute-start(f32[16,1152]{1,0:T(8,128)S(1)} %convolution_add_fusion.2), channel_id=1, source_target_pairs={{0,16},{16,32},{32,48},{48,64},{64,80},{80,96},{96,112},{112,128},... | collective-permute-start | bytes 221192 | tf_op jit(solution)/shard_map/while/body/eval_jaxpr/ppermute | solution.py:9
  327.9 11.6 %collective-permute-start = (bf16[16,1152]{1,0:T(8,128)(2,1)S(1)}, bf16[16,1152]{1,0:T(8,128)(2,1)S(1)}, u32[]{:S(2)}, u32[]{:S(2)}) collective-permute-start(bf16[16,1152]{1,0:T(8,128)(2,1)S(1)} %copy.20), channel_id=1, source_target_pairs={{0,16},{16,32},{32,48},{48,64},{64,80},{80,96},{96,112},{112,128},... | collective-permute-start | bytes 110600 | tf_op jit(solution)/shard_map/while/body/eval_jaxpr/ppermute | solution.py:9
  334.2 11.7 %collective-permute-start.1 = (f32[16,1152]{1,0:T(8,128)S(1)}, f32[16,1152]{1,0:T(8,128)S(1)}, u32[]{:S(2)}, u32[]{:S(2)}) collective-permute-start(f32[16,1152]{1,0:T(8,128)S(1)} %convolution_add_fusion.2), channel_id=1, source_target_pairs={{0,16},{16,32},{32,48},{48,64},{64,80},{80,96},{96,112},{112,128},... | collective-permute-start | bytes 221192 | tf_op jit(solution)/shard_map/while/body/eval_jaxpr/ppermute | solution.py:9
  345.9 11.6 %collective-permute-start = (bf16[16,1152]{1,0:T(8,128)(2,1)S(1)}, bf16[16,1152]{1,0:T(8,128)(2,1)S(1)}, u32[]{:S(2)}, u32[]{:S(2)}) collective-permute-start(bf16[16,1152]{1,0:T(8,128)(2,1)S(1)} %copy.20), channel_id=1, source_target_pairs={{0,16},{16,32},{32,48},{48,64},{64,80},{80,96},{96,112},{112,128},... | collective-permute-start | bytes 110600 | tf_op jit(solution)/shard_map/while/body/eval_jaxpr/ppermute | solution.py:9
  352.2 11.7 %collective-permute-start.1 = (f32[16,1152]{1,0:T(8,128)S(1)}, f32[16,1152]{1,0:T(8,128)S(1)}, u32[]{:S(2)}, u32[]{:S(2)}) collective-permute-start(f32[16,1152]{1,0:T(8,128)S(1)} %convolution_add_fusion.2), channel_id=1, source_target_pairs={{0,16},{16,32},{32,48},{48,64},{64,80},{80,96},{96,112},{112,128},... | collective-permute-start | bytes 221192 | tf_op jit(solution)/shard_map/while/body/eval_jaxpr/ppermute | solution.py:9
  363.9 11.6 %collective-permute-start = (bf16[16,1152]{1,0:T(8,128)(2,1)S(1)}, bf16[16,1152]{1,0:T(8,128)(2,1)S(1)}, u32[]{:S(2)}, u32[]{:S(2)}) collective-permute-start(bf16[16,1152]{1,0:T(8,128)(2,1)S(1)} %copy.20), channel_id=1, source_target_pairs={{0,16},{16,32},{32,48},{48,64},{64,80},{80,96},{96,112},{112,128},... | collective-permute-start | bytes 110600 | tf_op jit(solution)/shard_map/while/body/eval_jaxpr/ppermute | solution.py:9
  370.2 11.7 %collective-permute-start.1 = (f32[16,1152]{1,0:T(8,128)S(1)}, f32[16,1152]{1,0:T(8,128)S(1)}, u32[]{:S(2)}, u32[]{:S(2)}) collective-permute-start(f32[16,1152]{1,0:T(8,128)S(1)} %convolution_add_fusion.2), channel_id=1, source_target_pairs={{0,16},{16,32},{32,48},{48,64},{64,80},{80,96},{96,112},{112,128},... | collective-permute-start | bytes 221192 | tf_op jit(solution)/shard_map/while/body/eval_jaxpr/ppermute | solution.py:9
  381.9 11.6 %collective-permute-start = (bf16[16,1152]{1,0:T(8,128)(2,1)S(1)}, bf16[16,1152]{1,0:T(8,128)(2,1)S(1)}, u32[]{:S(2)}, u32[]{:S(2)}) collective-permute-start(bf16[16,1152]{1,0:T(8,128)(2,1)S(1)} %copy.20), channel_id=1, source_target_pairs={{0,16},{16,32},{32,48},{48,64},{64,80},{80,96},{96,112},{112,128},... | collective-permute-start | bytes 110600 | tf_op jit(solution)/shard_map/while/body/eval_jaxpr/ppermute | solution.py:9
  388.2 11.7 %collective-permute-start.1 = (f32[16,1152]{1,0:T(8,128)S(1)}, f32[16,1152]{1,0:T(8,128)S(1)}, u32[]{:S(2)}, u32[]{:S(2)}) collective-permute-start(f32[16,1152]{1,0:T(8,128)S(1)} %convolution_add_fusion.2), channel_id=1, source_target_pairs={{0,16},{16,32},{32,48},{48,64},{64,80},{80,96},{96,112},{112,128},... | collective-permute-start | bytes 221192 | tf_op jit(solution)/shard_map/while/body/eval_jaxpr/ppermute | solution.py:9
  399.9 11.6 %collective-permute-start = (bf16[16,1152]{1,0:T(8,128)(2,1)S(1)}, bf16[16,1152]{1,0:T(8,128)(2,1)S(1)}, u32[]{:S(2)}, u32[]{:S(2)}) collective-permute-start(bf16[16,1152]{1,0:T(8,128)(2,1)S(1)} %copy.20), channel_id=1, source_target_pairs={{0,16},{16,32},{32,48},{48,64},{64,80},{80,96},{96,112},{112,128},... | collective-permute-start | bytes 110600 | tf_op jit(solution)/shard_map/while/body/eval_jaxpr/ppermute | solution.py:9
  406.2 11.7 %collective-permute-start.1 = (f32[16,1152]{1,0:T(8,128)S(1)}, f32[16,1152]{1,0:T(8,128)S(1)}, u32[]{:S(2)}, u32[]{:S(2)}) collective-permute-start(f32[16,1152]{1,0:T(8,128)S(1)} %convolution_add_fusion.2), channel_id=1, source_target_pairs={{0,16},{16,32},{32,48},{48,64},{64,80},{80,96},{96,112},{112,128},... | collective-permute-start | bytes 221192 | tf_op jit(solution)/shard_map/while/body/eval_jaxpr/ppermute | solution.py:9
  417.9 11.6 %collective-permute-start = (bf16[16,1152]{1,0:T(8,128)(2,1)S(1)}, bf16[16,1152]{1,0:T(8,128)(2,1)S(1)}, u32[]{:S(2)}, u32[]{:S(2)}) collective-permute-start(bf16[16,1152]{1,0:T(8,128)(2,1)S(1)} %copy.20), channel_id=1, source_target_pairs={{0,16},{16,32},{32,48},{48,64},{64,80},{80,96},{96,112},{112,128},... | collective-permute-start | bytes 110600 | tf_op jit(solution)/shard_map/while/body/eval_jaxpr/ppermute | solution.py:9
  424.2 11.7 %collective-permute-start.1 = (f32[16,1152]{1,0:T(8,128)S(1)}, f32[16,1152]{1,0:T(8,128)S(1)}, u32[]{:S(2)}, u32[]{:S(2)}) collective-permute-start(f32[16,1152]{1,0:T(8,128)S(1)} %convolution_add_fusion.2), channel_id=1, source_target_pairs={{0,16},{16,32},{32,48},{48,64},{64,80},{80,96},{96,112},{112,128},... | collective-permute-start | bytes 221192 | tf_op jit(solution)/shard_map/while/body/eval_jaxpr/ppermute | solution.py:9
  435.9 11.6 %collective-permute-start = (bf16[16,1152]{1,0:T(8,128)(2,1)S(1)}, bf16[16,1152]{1,0:T(8,128)(2,1)S(1)}, u32[]{:S(2)}, u32[]{:S(2)}) collective-permute-start(bf16[16,1152]{1,0:T(8,128)(2,1)S(1)} %copy.20), channel_id=1, source_target_pairs={{0,16},{16,32},{32,48},{48,64},{64,80},{80,96},{96,112},{112,128},... | collective-permute-start | bytes 110600 | tf_op jit(solution)/shard_map/while/body/eval_jaxpr/ppermute | solution.py:9
  442.3 11.7 %collective-permute-start.1 = (f32[16,1152]{1,0:T(8,128)S(1)}, f32[16,1152]{1,0:T(8,128)S(1)}, u32[]{:S(2)}, u32[]{:S(2)}) collective-permute-start(f32[16,1152]{1,0:T(8,128)S(1)} %convolution_add_fusion.2), channel_id=1, source_target_pairs={{0,16},{16,32},{32,48},{48,64},{64,80},{80,96},{96,112},{112,128},... | collective-permute-start | bytes 221192 | tf_op jit(solution)/shard_map/while/body/eval_jaxpr/ppermute | solution.py:9
  454.0 11.6 %collective-permute-start = (bf16[16,1152]{1,0:T(8,128)(2,1)S(1)}, bf16[16,1152]{1,0:T(8,128)(2,1)S(1)}, u32[]{:S(2)}, u32[]{:S(2)}) collective-permute-start(bf16[16,1152]{1,0:T(8,128)(2,1)S(1)} %copy.20), channel_id=1, source_target_pairs={{0,16},{16,32},{32,48},{48,64},{64,80},{80,96},{96,112},{112,128},... | collective-permute-start | bytes 110600 | tf_op jit(solution)/shard_map/while/body/eval_jaxpr/ppermute | solution.py:9
  460.3 11.7 %collective-permute-start.1 = (f32[16,1152]{1,0:T(8,128)S(1)}, f32[16,1152]{1,0:T(8,128)S(1)}, u32[]{:S(2)}, u32[]{:S(2)}) collective-permute-start(f32[16,1152]{1,0:T(8,128)S(1)} %convolution_add_fusion.2), channel_id=1, source_target_pairs={{0,16},{16,32},{32,48},{48,64},{64,80},{80,96},{96,112},{112,128},... | collective-permute-start | bytes 221192 | tf_op jit(solution)/shard_map/while/body/eval_jaxpr/ppermute | solution.py:9
  472.0 11.6 %collective-permute-start = (bf16[16,1152]{1,0:T(8,128)(2,1)S(1)}, bf16[16,1152]{1,0:T(8,128)(2,1)S(1)}, u32[]{:S(2)}, u32[]{:S(2)}) collective-permute-start(bf16[16,1152]{1,0:T(8,128)(2,1)S(1)} %copy.20), channel_id=1, source_target_pairs={{0,16},{16,32},{32,48},{48,64},{64,80},{80,96},{96,112},{112,128},... | collective-permute-start | bytes 110600 | tf_op jit(solution)/shard_map/while/body/eval_jaxpr/ppermute | solution.py:9
  478.3 11.7 %collective-permute-start.1 = (f32[16,1152]{1,0:T(8,128)S(1)}, f32[16,1152]{1,0:T(8,128)S(1)}, u32[]{:S(2)}, u32[]{:S(2)}) collective-permute-start(f32[16,1152]{1,0:T(8,128)S(1)} %convolution_add_fusion.2), channel_id=1, source_target_pairs={{0,16},{16,32},{32,48},{48,64},{64,80},{80,96},{96,112},{112,128},... | collective-permute-start | bytes 221192 | tf_op jit(solution)/shard_map/while/body/eval_jaxpr/ppermute | solution.py:9
  490.0 11.6 %collective-permute-start = (bf16[16,1152]{1,0:T(8,128)(2,1)S(1)}, bf16[16,1152]{1,0:T(8,128)(2,1)S(1)}, u32[]{:S(2)}, u32[]{:S(2)}) collective-permute-start(bf16[16,1152]{1,0:T(8,128)(2,1)S(1)} %copy.20), channel_id=1, source_target_pairs={{0,16},{16,32},{32,48},{48,64},{64,80},{80,96},{96,112},{112,128},... | collective-permute-start | bytes 110600 | tf_op jit(solution)/shard_map/while/body/eval_jaxpr/ppermute | solution.py:9
  496.3 11.7 %collective-permute-start.1 = (f32[16,1152]{1,0:T(8,128)S(1)}, f32[16,1152]{1,0:T(8,128)S(1)}, u32[]{:S(2)}, u32[]{:S(2)}) collective-permute-start(f32[16,1152]{1,0:T(8,128)S(1)} %convolution_add_fusion.2), channel_id=1, source_target_pairs={{0,16},{16,32},{32,48},{48,64},{64,80},{80,96},{96,112},{112,128},... | collective-permute-start | bytes 221192 | tf_op jit(solution)/shard_map/while/body/eval_jaxpr/ppermute | solution.py:9
  508.0 11.6 %collective-permute-start = (bf16[16,1152]{1,0:T(8,128)(2,1)S(1)}, bf16[16,1152]{1,0:T(8,128)(2,1)S(1)}, u32[]{:S(2)}, u32[]{:S(2)}) collective-permute-start(bf16[16,1152]{1,0:T(8,128)(2,1)S(1)} %copy.20), channel_id=1, source_target_pairs={{0,16},{16,32},{32,48},{48,64},{64,80},{80,96},{96,112},{112,128},... | collective-permute-start | bytes 110600 | tf_op jit(solution)/shard_map/while/body/eval_jaxpr/ppermute | solution.py:9
  514.3 11.7 %collective-permute-start.1 = (f32[16,1152]{1,0:T(8,128)S(1)}, f32[16,1152]{1,0:T(8,128)S(1)}, u32[]{:S(2)}, u32[]{:S(2)}) collective-permute-start(f32[16,1152]{1,0:T(8,128)S(1)} %convolution_add_fusion.2), channel_id=1, source_target_pairs={{0,16},{16,32},{32,48},{48,64},{64,80},{80,96},{96,112},{112,128},... | collective-permute-start | bytes 221192 | tf_op jit(solution)/shard_map/while/body/eval_jaxpr/ppermute | solution.py:9
  526.0 12.0 %collective-permute-start = (bf16[16,1152]{1,0:T(8,128)(2,1)S(1)}, bf16[16,1152]{1,0:T(8,128)(2,1)S(1)}, u32[]{:S(2)}, u32[]{:S(2)}) collective-permute-start(bf16[16,1152]{1,0:T(8,128)(2,1)S(1)} %copy.20), channel_id=1, source_target_pairs={{0,16},{16,32},{32,48},{48,64},{64,80},{80,96},{96,112},{112,128},... | collective-permute-start | bytes 110600 | tf_op jit(solution)/shard_map/while/body/eval_jaxpr/ppermute | solution.py:9
  532.3 12.1 %collective-permute-start.1 = (f32[16,1152]{1,0:T(8,128)S(1)}, f32[16,1152]{1,0:T(8,128)S(1)}, u32[]{:S(2)}, u32[]{:S(2)}) collective-permute-start(f32[16,1152]{1,0:T(8,128)S(1)} %convolution_add_fusion.2), channel_id=1, source_target_pairs={{0,16},{16,32},{32,48},{48,64},{64,80},{80,96},{96,112},{112,128},... | collective-permute-start | bytes 221192 | tf_op jit(solution)/shard_map/while/body/eval_jaxpr/ppermute | solution.py:9
  544.4 12.0 %collective-permute-start = (bf16[16,1152]{1,0:T(8,128)(2,1)S(1)}, bf16[16,1152]{1,0:T(8,128)(2,1)S(1)}, u32[]{:S(2)}, u32[]{:S(2)}) collective-permute-start(bf16[16,1152]{1,0:T(8,128)(2,1)S(1)} %copy.20), channel_id=1, source_target_pairs={{0,16},{16,32},{32,48},{48,64},{64,80},{80,96},{96,112},{112,128},... | collective-permute-start | bytes 110600 | tf_op jit(solution)/shard_map/while/body/eval_jaxpr/ppermute | solution.py:9
  550.7 12.1 %collective-permute-start.1 = (f32[16,1152]{1,0:T(8,128)S(1)}, f32[16,1152]{1,0:T(8,128)S(1)}, u32[]{:S(2)}, u32[]{:S(2)}) collective-permute-start(f32[16,1152]{1,0:T(8,128)S(1)} %convolution_add_fusion.2), channel_id=1, source_target_pairs={{0,16},{16,32},{32,48},{48,64},{64,80},{80,96},{96,112},{112,128},... | collective-permute-start | bytes 221192 | tf_op jit(solution)/shard_map/while/body/eval_jaxpr/ppermute | solution.py:9
  562.8 12.0 %collective-permute-start = (bf16[16,1152]{1,0:T(8,128)(2,1)S(1)}, bf16[16,1152]{1,0:T(8,128)(2,1)S(1)}, u32[]{:S(2)}, u32[]{:S(2)}) collective-permute-start(bf16[16,1152]{1,0:T(8,128)(2,1)S(1)} %copy.20), channel_id=1, source_target_pairs={{0,16},{16,32},{32,48},{48,64},{64,80},{80,96},{96,112},{112,128},... | collective-permute-start | bytes 110600 | tf_op jit(solution)/shard_map/while/body/eval_jaxpr/ppermute | solution.py:9
  569.1 12.1 %collective-permute-start.1 = (f32[16,1152]{1,0:T(8,128)S(1)}, f32[16,1152]{1,0:T(8,128)S(1)}, u32[]{:S(2)}, u32[]{:S(2)}) collective-permute-start(f32[16,1152]{1,0:T(8,128)S(1)} %convolution_add_fusion.2), channel_id=1, source_target_pairs={{0,16},{16,32},{32,48},{48,64},{64,80},{80,96},{96,112},{112,128},... | collective-permute-start | bytes 221192 | tf_op jit(solution)/shard_map/while/body/eval_jaxpr/ppermute | solution.py:9
  581.2 12.0 %collective-permute-start = (bf16[16,1152]{1,0:T(8,128)(2,1)S(1)}, bf16[16,1152]{1,0:T(8,128)(2,1)S(1)}, u32[]{:S(2)}, u32[]{:S(2)}) collective-permute-start(bf16[16,1152]{1,0:T(8,128)(2,1)S(1)} %copy.20), channel_id=1, source_target_pairs={{0,16},{16,32},{32,48},{48,64},{64,80},{80,96},{96,112},{112,128},... | collective-permute-start | bytes 110600 | tf_op jit(solution)/shard_map/while/body/eval_jaxpr/ppermute | solution.py:9
  587.5 12.1 %collective-permute-start.1 = (f32[16,1152]{1,0:T(8,128)S(1)}, f32[16,1152]{1,0:T(8,128)S(1)}, u32[]{:S(2)}, u32[]{:S(2)}) collective-permute-start(f32[16,1152]{1,0:T(8,128)S(1)} %convolution_add_fusion.2), channel_id=1, source_target_pairs={{0,16},{16,32},{32,48},{48,64},{64,80},{80,96},{96,112},{112,128},... | collective-permute-start | bytes 221192 | tf_op jit(solution)/shard_map/while/body/eval_jaxpr/ppermute | solution.py:9
  599.6 12.0 %collective-permute-start = (bf16[16,1152]{1,0:T(8,128)(2,1)S(1)}, bf16[16,1152]{1,0:T(8,128)(2,1)S(1)}, u32[]{:S(2)}, u32[]{:S(2)}) collective-permute-start(bf16[16,1152]{1,0:T(8,128)(2,1)S(1)} %copy.20), channel_id=1, source_target_pairs={{0,16},{16,32},{32,48},{48,64},{64,80},{80,96},{96,112},{112,128},... | collective-permute-start | bytes 110600 | tf_op jit(solution)/shard_map/while/body/eval_jaxpr/ppermute | solution.py:9
  606.0 12.1 %collective-permute-start.1 = (f32[16,1152]{1,0:T(8,128)S(1)}, f32[16,1152]{1,0:T(8,128)S(1)}, u32[]{:S(2)}, u32[]{:S(2)}) collective-permute-start(f32[16,1152]{1,0:T(8,128)S(1)} %convolution_add_fusion.2), channel_id=1, source_target_pairs={{0,16},{16,32},{32,48},{48,64},{64,80},{80,96},{96,112},{112,128},... | collective-permute-start | bytes 221192 | tf_op jit(solution)/shard_map/while/body/eval_jaxpr/ppermute | solution.py:9
  618.0 11.9 %collective-permute-start = (bf16[16,1152]{1,0:T(8,128)(2,1)S(1)}, bf16[16,1152]{1,0:T(8,128)(2,1)S(1)}, u32[]{:S(2)}, u32[]{:S(2)}) collective-permute-start(bf16[16,1152]{1,0:T(8,128)(2,1)S(1)} %copy.20), channel_id=1, source_target_pairs={{0,16},{16,32},{32,48},{48,64},{64,80},{80,96},{96,112},{112,128},... | collective-permute-start | bytes 110600 | tf_op jit(solution)/shard_map/while/body/eval_jaxpr/ppermute | solution.py:9
  624.3 12.0 %collective-permute-start.1 = (f32[16,1152]{1,0:T(8,128)S(1)}, f32[16,1152]{1,0:T(8,128)S(1)}, u32[]{:S(2)}, u32[]{:S(2)}) collective-permute-start(f32[16,1152]{1,0:T(8,128)S(1)} %convolution_add_fusion.2), channel_id=1, source_target_pairs={{0,16},{16,32},{32,48},{48,64},{64,80},{80,96},{96,112},{112,128},... | collective-permute-start | bytes 221192 | tf_op jit(solution)/shard_map/while/body/eval_jaxpr/ppermute | solution.py:9
  (1 other events, 3.3 us)
Sparse Core Ops, SparseCore 0:
  638.0 84.2 reduce-scatter.1
where the time goes:
time: 759 us; the launch traced here: 754 us
  waiting for transfers between devices  264 us (35%)
  blocking collectives  152 us (20%)
  starting transfers between devices  134 us (18%)
  matrix products  101 us (13%)
  loops' own time  43.1 us (6%)
  other arithmetic  23.3 us (3%)
  local copies, waits for them, and re-layouts  21.7 us (3%)
  between operations  15.8 us (2%)
    ppermute x64, waiting for transfers between devices, from_behind(): lax.ppermute(x, axis, [(i, (i + by) % length) for i in range(length)])  264 us
    ppermute x64, starting transfers between devices, from_behind(): lax.ppermute(x, axis, [(i, (i + by) % length) for i in range(length)])  134 us
    psum x1, blocking collectives, local(): loss_all = lax.psum(loss_sum, ('wide', 'narrow'))  107 us
    dot_general x32, matrix products, pair_terms(): lax.dot_general(images, text_block, (((1,), (1,)), ((), ())), preferred_e...  71.3 us
    all_gather x1, blocking collectives, local(): images = lax.all_gather(image_embed, 'narrow', axis=0, tiled=True)  44.2 us
    another operation x1, loops' own time, local(): final_state, stacks = lax.scan(advance, start_state, hops)  43.1 us
    dot_general x32, matrix products, pair_terms(): lax.dot_general(weights, images, (((0,), (0,)), ((), ())), preferred_elem...  28 us
    dynamic_update_slice x32, other arithmetic, local(): final_state, stacks = lax.scan(advance, start_state, hops)  23 us
  transfers between devices with their start and end apart: 65, of which 61 were waited for; matrix products, arithmetic and copies ran while one was open for 19% of the time, Pallas kernels for 0%

commit v1 on v0

v1 whole, which is shorter than its diff:
```python
import functools

import jax
import jax.numpy as jnp
from jax import lax
from jax.experimental import pallas as pl
from jax.experimental.pallas import tpu as pltpu
from jax.sharding import PartitionSpec as P

MESH = pl.DeviceIdType.MESH
F32 = jnp.float32
BF16 = jnp.bfloat16
ROWS = 16
SET = 16 * ROWS
NT = (((1,), (1,)), ((), ()))


def place():
    wide = lax.axis_index("wide")
    narrow = lax.axis_index("narrow")
    return narrow // 4, (wide // 2) % 8, (wide // 16) * 4 + narrow % 4, wide % 2


def device(x, y, z, core):
    return ((z // 4) * 16 + y * 2 + core, x * 4 + z % 4)


def pair_weights(dots, scaling, offset, diagonal):
    logits = scaling * dots + offset
    if diagonal is None:
        turned = logits
    else:
        turned = jnp.where(diagonal, -logits, logits)
    small = jnp.exp(-jnp.abs(turned))
    chance = jnp.where(turned >= 0.0, 1.0, small) / (1.0 + small)
    weights = scaling * chance
    if diagonal is not None:
        weights = jnp.where(diagonal, -weights, weights)
    return turned, small, weights.astype(BF16)


def kernel(
    image_ref,
    text_ref,
    scale_ref,
    bias_ref,
    loss_ref,
    image_grad_ref,
    text_grad_ref,
    images,
    texts,
    weights,
    send_a,
    own_a,
    recv_a,
    send_b,
    recv_b,
    totals,
    first_send,
    first_recv,
    second_send,
    second_recv,
    sibling_send,
    sibling_recv,
    a_send,
    a_recv,
    b_send,
    b_recv,
    loss_send,
    loss_recv,
):
    x, y, z, core = place()
    scaling = scale_ref[0]
    offset = bias_ref[0]

    def along_x(k):
        return device((x + k) % 4, y, z, core)

    def along_y(k):
        return device(x, (y + 2 * k) % 8, z, core)

    def along_z(k):
        return device(x, y, (z + 2 * k) % 8, core)

    def in_block(k):
        flip_y, flip_z = k % 2, k // 2
        yy = y + flip_y * (1 - 2 * (y % 2))
        zz = z + flip_z * (1 - 2 * (z % 2))
        return device(x, yy, zz, core)

    def first_text(k):
        return device(x, (y + 2 * k * (1 - core)) % 8, (z + 2 * k * core) % 8, core)

    def second_text(k):
        return device(x, (y + 2 * k * core) % 8, (z + 2 * k * (1 - core)) % 8, core)

    sibling = device(x, y, z, 1 - core)

    def copy(src, dst, send, recv, to):
        made = pltpu.make_async_remote_copy(
            src_ref=src, dst_ref=dst, send_sem=send, recv_sem=recv, device_id=to, device_id_type=MESH
        )
        made.start()
        return made

    images[0:ROWS] = image_ref[...]
    texts[0:ROWS] = text_ref[...]

    barrier = pltpu.get_barrier_semaphore()
    for k in (1, 2, 3):
        for reach in (along_x, along_y, along_z, in_block):
            pl.semaphore_signal(barrier, inc=1, device_id=reach(k), device_id_type=MESH)
    pl.semaphore_signal(barrier, inc=1, device_id=sibling, device_id_type=MESH)
    pl.semaphore_wait(barrier, 13)

    sent = []
    first = []
    for k in (1, 2, 3):
        first.append(
            copy(
                texts.at[pl.ds(0, ROWS)],
                texts.at[pl.ds((4 - k) * ROWS, ROWS)],
                first_send.at[k - 1],
                first_recv.at[k - 1],
                first_text(k),
            )
        )
    for k in (1, 2, 3):
        first.append(
            copy(
                images.at[pl.ds(0, ROWS)],
                images.at[pl.ds(k * ROWS, ROWS)],
                first_send.at[2 + k],
                first_recv.at[2 + k],
                in_block(k),
            )
        )
    bundle = 4 * ROWS
    second = []
    for part, (array, reach) in enumerate(((images, along_x), (texts, second_text))):
        for made in first[3:] if part == 0 else first[:3]:
            made.wait_recv()
        for k in (1, 2, 3):
            second.append(
                copy(
                    array.at[pl.ds(0, bundle)],
                    array.at[pl.ds((4 - k) * bundle, bundle)],
                    second_send.at[3 * part + k - 1],
                    second_recv.at[3 * part + k - 1],
                    reach(k),
                )
            )
    sent += first + second
    shared = []
    for part, array in enumerate((images, texts)):
        for made in second[3 * part : 3 * part + 3]:
            made.wait_recv()
        shared.append(
            copy(
                array.at[pl.ds(0, SET)],
                array.at[pl.ds(SET, SET)],
                sibling_send.at[part],
                sibling_recv.at[part],
                sibling,
            )
        )
    sent += shared

    rows = lax.broadcasted_iota(jnp.int32, (SET, SET), 0)
    columns = lax.broadcasted_iota(jnp.int32, (SET, SET), 1)
    diagonal = (rows == columns) & (rows < ROWS)

    loss = jnp.zeros((8, 128), F32)
    partial = []
    for part, (mine, other) in enumerate(((images, texts), (texts, images))):
        for half in (0, 1):
            if half == 1:
                shared[1 - part].wait_recv()
            dots = lax.dot_general(
                mine[0:SET], other[half * SET : (half + 1) * SET], NT, preferred_element_type=F32
            )
            turned, small, tile = pair_weights(dots, scaling, offset, diagonal if half == 0 else None)
            weights[:, half * SET : (half + 1) * SET] = tile
            if part == 0:
                terms = jnp.maximum(turned, 0.0) + jnp.log1p(small)
                terms = jnp.sum(terms.reshape(SET // 8, 8, SET), axis=0)
                loss = loss + terms[:, 0:128] + terms[:, 128:256]
        grads = jnp.dot(weights[...], other[...], preferred_element_type=F32)
        own_a[part] = grads[0:bundle]
        send_a[part] = grads[bundle:].astype(BF16)
        reach = along_x if part == 0 else second_text
        for k in (1, 2, 3):
            partial.append(
                copy(
                    send_a.at[part, pl.ds((k - 1) * bundle, bundle)],
                    recv_a.at[part, 3 - k],
                    a_send.at[part, k - 1],
                    a_recv.at[part, k - 1],
                    reach(k),
                )
            )
    sent += partial

    stages = (
        (core, (1,), lambda k: sibling),
        (x, (1, 2, 3), along_x),
        ((y % 2) + 2 * (z % 2), (1, 2, 3), in_block),
        (y // 2, (1, 2, 3), along_y),
        (z // 2, (1, 2, 3), along_z),
    )

    def give(stage, value):
        slot, steps, reach = stages[stage]
        totals[stage, slot] = value
        return [
            copy(
                totals.at[stage, slot],
                totals.at[stage, slot],
                loss_send.at[stage, k - 1],
                loss_recv.at[stage, k - 1],
                reach(k),
            )
            for k in steps
        ]

    def take(stage, gifts):
        for made in gifts:
            made.wait_recv()
        sent.extend(gifts)
        value = totals[stage, 0] + totals[stage, 1]
        if stage > 0:
            value = value + totals[stage, 2] + totals[stage, 3]
        return value

    loss = take(0, give(0, loss))
    gifts = give(1, loss)

    last = []
    for part in (0, 1):
        for made in partial[3 * part : 3 * part + 3]:
            made.wait_recv()
        total = own_a[part]
        for k in range(3):
            total = total + recv_a[part, k].astype(F32)
        send_b[part] = total
        reach = in_block if part == 0 else first_text
        for k in (1, 2, 3):
            last.append(
                copy(
                    send_b.at[part, pl.ds(k * ROWS, ROWS)],
                    recv_b.at[part, k - 1 if part == 0 else 3 - k],
                    b_send.at[part, k - 1],
                    b_recv.at[part, k - 1],
                    reach(k),
                )
            )
        loss = take(1 + part, gifts)
        gifts = give(2 + part, loss)
    loss = take(3, gifts)
    gifts = give(4, loss)
    sent += last
    for part, out in enumerate((image_grad_ref, text_grad_ref)):
        for made in last[3 * part : 3 * part + 3]:
            made.wait_recv()
        total = send_b[part, 0:ROWS]
        for k in range(3):
            total = total + recv_b[part, k]
        out[...] = total
    loss = take(4, gifts)
    loss_ref[0] = jnp.sum(loss) / 8192.0
    for made in sent:
        made.wait_send()


def local(image_embed, text_embed, logit_scale, logit_bias):
    width = image_embed.shape[1]
    vmem = pl.BlockSpec(memory_space=pltpu.VMEM)
    smem = pl.BlockSpec(memory_space=pltpu.SMEM)
    dma = pltpu.SemaphoreType.DMA
    grad = jax.ShapeDtypeStruct((ROWS, width), F32)
    return pl.pallas_call(
        kernel,
        out_shape=(jax.ShapeDtypeStruct((1,), F32), grad, grad),
        in_specs=[vmem, vmem, smem, smem],
        out_specs=(smem, vmem, vmem),
        scratch_shapes=[
            pltpu.VMEM((2 * SET, width), BF16),
            pltpu.VMEM((2 * SET, width), BF16),
            pltpu.VMEM((SET, 2 * SET), BF16),
            pltpu.VMEM((2, 12 * ROWS, width), BF16),
            pltpu.VMEM((2, 4 * ROWS, width), F32),
            pltpu.VMEM((2, 3, 4 * ROWS, width), BF16),
            pltpu.VMEM((2, 4 * ROWS, width), F32),
            pltpu.VMEM((2, 3, ROWS, width), F32),
            pltpu.VMEM((5, 4, 8, 128), F32),
            dma((6,)),
            dma((6,)),
            dma((6,)),
            dma((6,)),
            dma((2,)),
            dma((2,)),
            dma((2, 3)),
            dma((2, 3)),
            dma((2, 3)),
            dma((2, 3)),
            dma((5, 3)),
            dma((5, 3)),
        ],
        compiler_params=pltpu.CompilerParams(
            collective_id=0, has_side_effects=True, vmem_limit_bytes=48 * 2**20
        ),
        name="pairs",
    )(image_embed, text_embed, logit_scale, logit_bias)


def solution(mesh):
    rows = P(("wide", "narrow"), None)
    return jax.shard_map(
        local, mesh=mesh, in_specs=(rows, rows, P(), P()), out_specs=(P(), rows, rows), check_vma=False
    )
```

time: 759 us -> 65.1 us (0.09)
  waiting for transfers between devices: 264 us -> 0 us
  blocking collectives: 152 us -> 0 us
  starting transfers between devices: 134 us -> 0 us
  matrix products: 101 us -> 0 us
  Pallas kernels: 0 us -> 58.3 us
  loops' own time: 43.1 us -> 0 us
  other arithmetic: 23.3 us -> 0 us
  local copies, waits for them, and re-layouts: 21.7 us -> 2.8 us
  between operations: 15.8 us -> 3.7 us
    ppermute x64 -> x0, waiting for transfers between devices: 264 us -> none  [from_behind(): lax.ppermute(x, axis, [(i, (i + by) % length) for i in range(length)])]
    ppermute x64 -> x0, starting transfers between devices: 134 us -> none  [from_behind(): lax.ppermute(x, axis, [(i, (i + by) % length) for i in range(length)])]
    psum x1 -> x0, blocking collectives: 107 us -> none  [local(): loss_all = lax.psum(loss_sum, ('wide', 'narrow'))]
    dot_general x65 -> x0, matrix products: 101 us -> none  [the longest x32 71.3 us: pair_terms(): lax.dot_general(images, text_block, (((1,), (1,)), ((), ())), preferred_e...]
    pallas_call x0 -> x1, Pallas kernels: none -> 58.3 us  [local(): pl.pallas_call(kernel, out_shape=(jax.ShapeDtypeStruct((1,), F32), grad,...]
    all_gather x1 -> x0, blocking collectives: 44.2 us -> none  [local(): images = lax.all_gather(image_embed, 'narrow', axis=0, tiled=True)]
    another operation x1 -> x0, loops' own time: 43.1 us -> none  [local(): final_state, stacks = lax.scan(advance, start_state, hops)]
    dynamic_update_slice x32 -> x0, other arithmetic: 23 us -> none  [local(): final_state, stacks = lax.scan(advance, start_state, hops)]
  transfers between devices with their start and end apart: 65 -> 0, of which waited for: 61 -> 0; matrix products, arithmetic and copies ran while one was open for 19% -> 0% of each run, Pallas kernels for 0% -> 0%
where the time goes in v1:
time: 65.1 us; the launch traced here: 64.8 us
  Pallas kernels  58.3 us (90%)
  between operations  3.7 us (6%)
  local copies, waits for them, and re-layouts  2.8 us (4%)
    pallas_call x1, Pallas kernels, local(): pl.pallas_call(kernel, out_shape=(jax.ShapeDtypeStruct((1,), F32), grad,...  58.3 us
    unnamed x6, local copies, waits for them, and re-layouts  2.8 us

profile of v1, /device:TPU:1, one launch (start us, length us, event | category | flops | bytes accessed | tf_op | source)
XLA Modules:
  0.0 64.8 jit_solution(15080029817579573763)
XLA Ops:
  1.9 0.0 copy-start
  1.9 0.8 %copy-done = bf16[16,1152]{1,0:T(8,128)(2,1)S(1)} copy-done((bf16[16,1152]{1,0:T(8,128)(2,1)S(1)}, bf16[16,1152]{1,0:T(8,128)(2,1)}, u32[]{:S(2)}) %copy-start) | copy-done | bytes 36888
  2.7 0.0 copy-start.1
  2.7 0.8 %copy-done.1 = bf16[16,1152]{1,0:T(8,128)(2,1)S(1)} copy-done((bf16[16,1152]{1,0:T(8,128)(2,1)S(1)}, bf16[16,1152]{1,0:T(8,128)(2,1)}, u32[]{:S(2)}) %copy-start.1) | copy-done | bytes 36888
  3.5 58.3 %pairs.1 = (f32[1]{0:T(128)}, f32[16,1152]{1,0:T(8,128)S(1)}, f32[16,1152]{1,0:T(8,128)S(1)}) custom-call(bf16[16,1152]{1,0:T(8,128)(2,1)S(1)} %copy-done, bf16[16,1152]{1,0:T(8,128)(2,1)S(1)} %copy-done.1, f32[1]{0:T(128)S(6)} %copy.10.scale_ref, f32[1]{0:T(128)S(6)} %copy.11.bias_ref), custom_call_target="tpu_custom_call" | custom-call | tf_op jit(solution)/shard_map/pairs/pallas_call | solution.py:281
  62.4 0.6 copy.13
  63.0 0.6 copy.14
Async XLA Ops:
  1.9 0.8 %copy-start = (bf16[16,1152]{1,0:T(8,128)(2,1)S(1)}, bf16[16,1152]{1,0:T(8,128)(2,1)}, u32[]{:S(2)}) copy-start(bf16[16,1152]{1,0:T(8,128)(2,1)} %image_ref.1) | copy-start | bytes 110596
  2.7 0.8 %copy-start.1 = (bf16[16,1152]{1,0:T(8,128)(2,1)S(1)}, bf16[16,1152]{1,0:T(8,128)(2,1)}, u32[]{:S(2)}) copy-start(bf16[16,1152]{1,0:T(8,128)(2,1)} %text_ref.1) | copy-start | bytes 110596

commit v2 on v1

v2 whole, which is shorter than its diff:
```python
import jax
import jax.numpy as jnp
from jax import lax
from jax.experimental import pallas as pl
from jax.experimental.pallas import tpu as pltpu
from jax.sharding import PartitionSpec as P

MESH = pl.DeviceIdType.MESH
F32 = jnp.float32
BF16 = jnp.bfloat16
ROWS = 16
SET = 16 * ROWS
CUT = 640
NT = (((1,), (1,)), ((), ()))


def place():
    wide = lax.axis_index("wide")
    narrow = lax.axis_index("narrow")
    return narrow // 4, (wide // 2) % 8, (wide // 16) * 4 + narrow % 4, wide % 2


def device(x, y, z, core):
    return ((z // 4) * 16 + y * 2 + core, x * 4 + z % 4)


def pair_weights(dots, scaling, offset, diagonal):
    logits = scaling * dots + offset
    if diagonal is None:
        turned = logits
    else:
        turned = jnp.where(diagonal, -logits, logits)
    small = jnp.exp(-jnp.abs(turned))
    chance = jnp.where(turned >= 0.0, 1.0, small) / (1.0 + small)
    weights = scaling * chance
    if diagonal is not None:
        weights = jnp.where(diagonal, -weights, weights)
    return turned, small, weights.astype(BF16)


def kernel(
    image_ref,
    text_ref,
    scale_ref,
    bias_ref,
    loss_ref,
    image_grad_ref,
    text_grad_ref,
    images,
    texts,
    weights,
    text_parts,
    text_near,
    text_far,
    text_own,
    came_z,
    came_y,
    last_y,
    last_z,
    image_parts,
    image_own,
    came_x,
    block_parts,
    last_block,
    totals,
    load,
    near_send,
    near_recv,
    far_send,
    far_recv,
    image_send,
    image_recv,
    sibling_send,
    sibling_recv,
    a_send,
    a_recv,
    b_send,
    b_recv,
    image_a_send,
    image_a_recv,
    image_b_send,
    image_b_recv,
    loss_send,
    loss_recv,
):
    x, y, z, core = place()
    steps = (2, 1, 3)

    def along_x(k):
        return device((x + k) % 4, y, z, core)

    def along_y(k):
        return device(x, (y + 2 * k) % 8, z, core)

    def along_z(k):
        return device(x, y, (z + 2 * k) % 8, core)

    def in_block(k):
        flip_y, flip_z = k % 2, k // 2
        yy = y + flip_y * (1 - 2 * (y % 2))
        zz = z + flip_z * (1 - 2 * (z % 2))
        return device(x, yy, zz, core)

    sibling = device(x, y, z, 1 - core)

    sent = []

    def copy(src, dst, send, recv, to):
        made = pltpu.make_async_remote_copy(
            src_ref=src, dst_ref=dst, send_sem=send, recv_sem=recv, device_id=to, device_id_type=MESH
        )
        made.start()
        sent.append(made)
        return made

    def arrived(copies):
        for made in copies:
            made.wait_recv()

    loads = [
        pltpu.make_async_copy(text_ref, texts.at[0, 0, 0], load.at[0]),
        pltpu.make_async_copy(image_ref, images.at[pl.ds(0, ROWS)], load.at[1]),
    ]
    for made in loads:
        made.start()
    barrier = pltpu.get_barrier_semaphore()
    for k in steps:
        for reach in (along_y, along_z, along_x, in_block):
            pl.semaphore_signal(barrier, inc=1, device_id=reach(k), device_id_type=MESH)
    pl.semaphore_signal(barrier, inc=1, device_id=sibling, device_id_type=MESH)
    scaling = scale_ref[0]
    offset = bias_ref[0]
    for made in loads:
        made.wait()
    pl.semaphore_wait(barrier, 13)

    from_y, from_z, from_block = [], [], []
    mine = texts.at[0, 0, 0]
    for k in steps:
        from_y.append(copy(mine, texts.at[0, 0, 4 - k], near_send.at[0, k - 1], near_recv.at[0, k - 1], along_y(k)))
        from_z.append(copy(mine, texts.at[0, 4 - k, 0], near_send.at[1, k - 1], near_recv.at[1, k - 1], along_z(k)))
    own = images.at[pl.ds(0, ROWS)]
    for k in steps:
        from_block.append(
            copy(own, images.at[pl.ds(k * ROWS, ROWS)], image_send.at[0, k - 1], image_recv.at[0, k - 1], in_block(k))
        )
    arrived(from_block)
    from_x = []
    bundle = 4 * ROWS
    for k in steps:
        from_x.append(
            copy(
                images.at[pl.ds(0, bundle)],
                images.at[pl.ds((4 - k) * bundle, bundle)],
                image_send.at[1, k - 1],
                image_recv.at[1, k - 1],
                along_x(k),
            )
        )
    head, tail = pl.ds(0, CUT), pl.ds(CUT, texts.shape[-1] - CUT)
    rest = pl.ds(1, 3)
    arrived(from_y)
    passed = []
    for k in steps:
        passed.append(
            copy(
                texts.at[0, 0, rest, :, head],
                texts.at[0, 4 - k, rest, :, head],
                far_send.at[0, k - 1],
                far_recv.at[0, k - 1],
                along_z(k),
            )
        )
    arrived(from_z)
    for k in steps:
        passed.append(
            copy(
                texts.at[0, rest, 0, :, tail],
                texts.at[0, rest, 4 - k, :, tail],
                far_send.at[1, k - 1],
                far_recv.at[1, k - 1],
                along_y(k),
            )
        )
    arrived(from_x)
    image_share = copy(
        images.at[pl.ds(0, SET)], images.at[pl.ds(SET, SET)], sibling_send.at[0], sibling_recv.at[0], sibling
    )
    arrived(passed)
    text_share = copy(texts.at[0], texts.at[1], sibling_send.at[1], sibling_recv.at[1], sibling)

    rows = lax.broadcasted_iota(jnp.int32, (SET, SET), 0)
    columns = lax.broadcasted_iota(jnp.int32, (SET, SET), 1)
    diagonal = (rows == columns) & (rows < ROWS)

    stages = (
        (core, (1,), lambda k: sibling),
        (x, steps, along_x),
        ((y % 2) + 2 * (z % 2), steps, in_block),
        (y // 2, steps, along_y),
        (z // 2, steps, along_z),
    )

    def give(stage, value):
        slot, ways, reach = stages[stage]
        totals[stage, slot] = value
        return [
            copy(
                totals.at[stage, slot],
                totals.at[stage, slot],
                loss_send.at[stage, k - 1],
                loss_recv.at[stage, k - 1],
                reach(k),
            )
            for k in ways
        ]

    def take(stage, gifts):
        arrived(gifts)
        value = totals[stage, 0] + totals[stage, 1]
        if stage > 0:
            value = value + totals[stage, 2] + totals[stage, 3]
        return value

    def text_set(half):
        return texts[half].reshape(SET, texts.shape[-1])

    loss = jnp.zeros((8, 128), F32)
    for half in (0, 1):
        if half == 1:
            image_share.wait_recv()
        dots = lax.dot_general(
            text_set(0), images[half * SET : (half + 1) * SET], NT, preferred_element_type=F32
        )
        turned, small, tile = pair_weights(dots, scaling, offset, diagonal if half == 0 else None)
        weights[:, half * SET : (half + 1) * SET] = tile
        terms = jnp.maximum(turned, 0.0) + jnp.log1p(small)
        terms = jnp.sum(terms.reshape(SET // 8, 8, SET), axis=0)
        loss = loss + terms[:, 0:128] + terms[:, 128:256]
    gifts = give(0, loss)
    grads = jnp.dot(weights[...], images[...], preferred_element_type=F32).reshape(4, 4, ROWS, -1)
    text_parts[...] = grads.astype(BF16)
    text_near[...] = grads[0, 1:4, :, 0:CUT]
    text_far[...] = grads[1:4, 0, :, CUT:]
    text_own[...] = grads[0, 0]
    to_z, to_y = [], []
    for k in steps:
        to_z.append(
            copy(
                text_parts.at[k, rest, :, head], came_z.at[3 - k], a_send.at[0, k - 1], a_recv.at[0, k - 1], along_z(k)
            )
        )
        to_y.append(
            copy(
                text_parts.at[rest, k, :, tail], came_y.at[3 - k], a_send.at[1, k - 1], a_recv.at[1, k - 1], along_y(k)
            )
        )
    gifts = give(1, take(0, gifts))

    text_share.wait_recv()
    for half in (0, 1):
        dots = lax.dot_general(images[0:SET], text_set(half), NT, preferred_element_type=F32)
        weights[:, half * SET : (half + 1) * SET] = pair_weights(
            dots, scaling, offset, diagonal if half == 0 else None
        )[2]
    grads = jnp.dot(
        weights[...], texts[...].reshape(2 * SET, texts.shape[-1]), preferred_element_type=F32
    )
    image_own[...] = grads[0:bundle]
    image_parts[...] = grads[bundle:].astype(BF16)
    to_x = []
    for k in steps:
        to_x.append(
            copy(
                image_parts.at[pl.ds((k - 1) * bundle, bundle)],
                came_x.at[3 - k],
                image_a_send.at[k - 1],
                image_a_recv.at[k - 1],
                along_x(k),
            )
        )
    gifts = give(2, take(1, gifts))

    arrived(to_z)
    total = text_near[...]
    for k in range(3):
        total = total + came_z[k].astype(F32)
    text_parts[0, 1:4, :, 0:CUT] = total.astype(BF16)
    out_y, out_z, out_block = [], [], []
    for k in steps:
        out_y.append(
            copy(text_parts.at[0, k], last_y.at[3 - k], b_send.at[0, k - 1], b_recv.at[0, k - 1], along_y(k))
        )
    arrived(to_y)
    total = text_far[...]
    for k in range(3):
        total = total + came_y[k].astype(F32)
    text_parts[1:4, 0, :, CUT:] = total.astype(BF16)
    for k in steps:
        out_z.append(
            copy(text_parts.at[k, 0], last_z.at[3 - k], b_send.at[1, k - 1], b_recv.at[1, k - 1], along_z(k))
        )
    gifts = give(3, take(2, gifts))
    arrived(to_x)
    total = image_own[...]
    for k in range(3):
        total = total + came_x[k].astype(F32)
    image_own[0:ROWS] = total[0:ROWS]
    block_parts[...] = total[ROWS:].astype(BF16)
    for k in steps:
        out_block.append(
            copy(
                block_parts.at[pl.ds((k - 1) * ROWS, ROWS)],
                last_block.at[k - 1],
                image_b_send.at[k - 1],
                image_b_recv.at[k - 1],
                in_block(k),
            )
        )
    gifts = give(4, take(3, gifts))
    arrived(out_block)
    total = image_own[0:ROWS]
    for k in range(3):
        total = total + last_block[k].astype(F32)
    image_grad_ref[...] = total
    arrived(out_y + out_z)
    total = text_own[...]
    for k in range(3):
        total = total + last_y[k].astype(F32) + last_z[k].astype(F32)
    text_grad_ref[...] = total
    loss_ref[0] = jnp.sum(take(4, gifts)) / 8192.0
    for made in sent:
        made.wait_send()


def local(image_embed, text_embed, logit_scale, logit_bias):
    width = image_embed.shape[1]
    vmem = pl.BlockSpec(memory_space=pltpu.VMEM)
    smem = pl.BlockSpec(memory_space=pltpu.SMEM)
    hbm = pl.BlockSpec(memory_space=pltpu.HBM)
    dma = pltpu.SemaphoreType.DMA
    grad = jax.ShapeDtypeStruct((ROWS, width), F32)
    return pl.pallas_call(
        kernel,
        out_shape=(jax.ShapeDtypeStruct((1,), F32), grad, grad),
        in_specs=[hbm, hbm, smem, smem],
        out_specs=(smem, vmem, vmem),
        scratch_shapes=[
            pltpu.VMEM((2 * SET, width), BF16),
            pltpu.VMEM((2, 4, 4, ROWS, width), BF16),
            pltpu.VMEM((SET, 2 * SET), BF16),
            pltpu.VMEM((4, 4, ROWS, width), BF16),
            pltpu.VMEM((3, ROWS, CUT), F32),
            pltpu.VMEM((3, ROWS, width - CUT), F32),
            pltpu.VMEM((ROWS, width), F32),
            pltpu.VMEM((3, 3, ROWS, CUT), BF16),
            pltpu.VMEM((3, 3, ROWS, width - CUT), BF16),
            pltpu.VMEM((3, ROWS, width), BF16),
            pltpu.VMEM((3, ROWS, width), BF16),
            pltpu.VMEM((12 * ROWS, width), BF16),
            pltpu.VMEM((4 * ROWS, width), F32),
            pltpu.VMEM((3, 4 * ROWS, width), BF16),
            pltpu.VMEM((3 * ROWS, width), BF16),
            pltpu.VMEM((3, ROWS, width), BF16),
            pltpu.VMEM((5, 4, 8, 128), F32),
            dma((2,)),
            dma((2, 3)),
            dma((2, 3)),
            dma((2, 3)),
            dma((2, 3)),
            dma((2, 3)),
            dma((2, 3)),
            dma((2,)),
            dma((2,)),
            dma((2, 3)),
            dma((2, 3)),
            dma((2, 3)),
            dma((2, 3)),
            dma((3,)),
            dma((3,)),
            dma((3,)),
            dma((3,)),
            dma((5, 3)),
            dma((5, 3)),
        ],
        compiler_params=pltpu.CompilerParams(
            collective_id=0, has_side_effects=True, vmem_limit_bytes=60 * 2**20
        ),
        name="pairs",
    )(image_embed, text_embed, logit_scale, logit_bias)


def solution(mesh):
    rows = P(("wide", "narrow"), None)
    return jax.shard_map(
        local, mesh=mesh, in_specs=(rows, rows, P(), P()), out_specs=(P(), rows, rows), check_vma=False
    )
```

time: 65.1 us -> 59.3 us (0.911)
  Pallas kernels: 58.3 us -> 53 us
    pallas_call x1, Pallas kernels: 58.3 us -> 53 us  [local(): pl.pallas_call(kernel, out_shape=(jax.ShapeDtypeStruct((1,), F32), grad,...]
    unnamed x6 -> x4, local copies, waits for them, and re-layouts: 2.8 us -> 2.19 us
where the time goes in v2:
time: 59.3 us; the launch traced here: 58.8 us
  Pallas kernels  53 us (89%)
  between operations  3.69 us (6%)
  local copies, waits for them, and re-layouts  2.19 us (4%)
    pallas_call x1, Pallas kernels, local(): pl.pallas_call(kernel, out_shape=(jax.ShapeDtypeStruct((1,), F32), grad,...  53 us
    unnamed x4, local copies, waits for them, and re-layouts  2.19 us

profile of v2, /device:TPU:1, one launch (start us, length us, event | category | flops | bytes accessed | tf_op | source)
XLA Modules:
  0.0 58.8 jit_solution(8361896652792069392)
XLA Ops:
  1.9 53.0 %pairs.1 = (f32[1]{0:T(128)}, f32[16,1152]{1,0:T(8,128)}, f32[16,1152]{1,0:T(8,128)}) custom-call(bf16[16,1152]{1,0:T(8,128)(2,1)} %image_ref.1, bf16[16,1152]{1,0:T(8,128)(2,1)} %text_ref.1, f32[1]{0:T(128)S(6)} %copy.10.scale_ref, f32[1]{0:T(128)S(6)} %copy.11.bias_ref), custom_call_target="tpu_custom_call" | custom-call | tf_op jit(solution)/shard_map/pairs/pallas_call | solution.py:343
  55.5 0.0 copy-start
  55.5 1.6 %copy.13 = f32[16,1152]{1,0:T(8,128)} copy(f32[16,1152]{1,0:T(8,128)} %get-tuple-element.7) | data formatting | bytes 147456
  57.1 0.0 copy-done
  57.1 0.6 %copy.14 = f32[16,1152]{1,0:T(8,128)} copy(f32[16,1152]{1,0:T(8,128)S(1)} %copy-done) | data formatting | bytes 147456
Async XLA Ops:
  55.5 1.6 %copy-start = (f32[16,1152]{1,0:T(8,128)S(1)}, f32[16,1152]{1,0:T(8,128)}, u32[]{:S(2)}) copy-start(f32[16,1152]{1,0:T(8,128)} %get-tuple-element.8) | copy-start | bytes 221188

commit v3 on v2

--- a/solution.py
+++ b/solution.py
@@ -17,11 +17,13 @@
 def place():
     wide = lax.axis_index("wide")
     narrow = lax.axis_index("narrow")
-    return narrow // 4, (wide // 2) % 8, (wide // 16) * 4 + narrow % 4, wide % 2
+    y = lax.rem(lax.div(wide, 2), 8)
+    z = lax.div(wide, 16) * 4 + lax.rem(narrow, 4)
+    return lax.div(narrow, 4), y, z, lax.rem(wide, 2)
 
 
 def device(x, y, z, core):
-    return ((z // 4) * 16 + y * 2 + core, x * 4 + z % 4)
+    return (lax.div(z, 4) * 16 + y * 2 + core, x * 4 + lax.rem(z, 4))
 
 
 def pair_weights(dots, scaling, offset, diagonal):
@@ -63,6 +65,7 @@
     block_parts,
     last_block,
     totals,
+    numbers,
     load,
     near_send,
     near_recv,
@@ -86,22 +89,32 @@
     x, y, z, core = place()
     steps = (2, 1, 3)
 
+    flipped_y = y + 1 - 2 * lax.rem(y, 2)
+    flipped_z = z + 1 - 2 * lax.rem(z, 2)
+    all_steps = (4, 3, 5, 2, 6, 1, 7)
+
     def along_x(k):
-        return device((x + k) % 4, y, z, core)
+        return device(lax.rem(x + k, 4), y, z, core)
+
+    def ring_y(k):
+        return device(x, lax.rem(y + k, 8), z, core)
+
+    def ring_z(k):
+        return device(x, y, lax.rem(z + k, 8), core)
 
     def along_y(k):
-        return device(x, (y + 2 * k) % 8, z, core)
+        return ring_y(2 * k)
 
     def along_z(k):
-        return device(x, y, (z + 2 * k) % 8, core)
+        return ring_z(2 * k)
+
+    def in_row(k):
+        return device(lax.rem(x + k // 2, 4), y, z, 1 - core if k % 2 else core)
 
     def in_block(k):
-        flip_y, flip_z = k % 2, k // 2
-        yy = y + flip_y * (1 - 2 * (y % 2))
-        zz = z + flip_z * (1 - 2 * (z % 2))
-        return device(x, yy, zz, core)
-
-    sibling = device(x, y, z, 1 - core)
+        return device(x, flipped_y if k % 2 else y, flipped_z if k // 2 else z, core)
+
+    sibling = in_row(1)
 
     sent = []
 
@@ -117,33 +130,35 @@
         for made in copies:
             made.wait_recv()
 
+    barrier = pltpu.get_barrier_semaphore()
+    for reach in (ring_y, ring_z, in_row):
+        for k in all_steps:
+            pl.semaphore_signal(barrier, inc=1, device_id=reach(k), device_id_type=MESH)
+    pl.semaphore_signal(barrier, inc=1, device_id=in_block(3), device_id_type=MESH)
     loads = [
-        pltpu.make_async_copy(text_ref, texts.at[0, 0, 0], load.at[0]),
-        pltpu.make_async_copy(image_ref, images.at[pl.ds(0, ROWS)], load.at[1]),
+        pltpu.make_async_copy(image_ref, images.at[pl.ds(0, ROWS)], load.at[0]),
+        pltpu.make_async_copy(text_ref, texts.at[0, 0, 0], load.at[1]),
+        pltpu.make_async_copy(scale_ref, numbers.at[0], load.at[2]),
+        pltpu.make_async_copy(bias_ref, numbers.at[1], load.at[3]),
     ]
     for made in loads:
         made.start()
-    barrier = pltpu.get_barrier_semaphore()
-    for k in steps:
-        for reach in (along_y, along_z, along_x, in_block):
-            pl.semaphore_signal(barrier, inc=1, device_id=reach(k), device_id_type=MESH)
-    pl.semaphore_signal(barrier, inc=1, device_id=sibling, device_id_type=MESH)
-    scaling = scale_ref[0]
-    offset = bias_ref[0]
     for made in loads:
         made.wait()
-    pl.semaphore_wait(barrier, 13)
+    scaling = numbers[0, 0]
+    offset = numbers[1, 0]
+    pl.semaphore_wait(barrier, 22)
 
     from_y, from_z, from_block = [], [], []
+    own = images.at[pl.ds(0, ROWS)]
+    for k in steps:
+        from_block.append(
+            copy(own, images.at[pl.ds(k * ROWS, ROWS)], image_send.at[0, k - 1], image_recv.at[0, k - 1], in_block(k))
+        )
     mine = texts.at[0, 0, 0]
     for k in steps:
         from_y.append(copy(mine, texts.at[0, 0, 4 - k], near_send.at[0, k - 1], near_recv.at[0, k - 1], along_y(k)))
         from_z.append(copy(mine, texts.at[0, 4 - k, 0], near_send.at[1, k - 1], near_recv.at[1, k - 1], along_z(k)))
-    own = images.at[pl.ds(0, ROWS)]
-    for k in steps:
-        from_block.append(
-            copy(own, images.at[pl.ds(k * ROWS, ROWS)], image_send.at[0, k - 1], image_recv.at[0, k - 1], in_block(k))
-        )
     arrived(from_block)
     from_x = []
     bundle = 4 * ROWS
@@ -193,33 +208,30 @@
     columns = lax.broadcasted_iota(jnp.int32, (SET, SET), 1)
     diagonal = (rows == columns) & (rows < ROWS)
 
-    stages = (
-        (core, (1,), lambda k: sibling),
-        (x, steps, along_x),
-        ((y % 2) + 2 * (z % 2), steps, in_block),
-        (y // 2, steps, along_y),
-        (z // 2, steps, along_z),
-    )
+    stages = ((y, ring_y), (z, ring_z), (2 * x + core, in_row))
+
+    def way_back(stage, k):
+        return 8 - k if stage < 2 else (8 - k // 2 * 2) % 8 + k % 2
 
     def give(stage, value):
-        slot, ways, reach = stages[stage]
+        slot, reach = stages[stage]
         totals[stage, slot] = value
         return [
             copy(
                 totals.at[stage, slot],
                 totals.at[stage, slot],
                 loss_send.at[stage, k - 1],
-                loss_recv.at[stage, k - 1],
+                loss_recv.at[stage, way_back(stage, k) - 1],
                 reach(k),
             )
-            for k in ways
+            for k in all_steps
         ]
 
     def take(stage, gifts):
         arrived(gifts)
-        value = totals[stage, 0] + totals[stage, 1]
-        if stage > 0:
-            value = value + totals[stage, 2] + totals[stage, 3]
+        value = totals[stage, 0]
+        for k in range(1, 8):
+            value = value + totals[stage, k]
         return value
 
     def text_set(half):
@@ -255,7 +267,6 @@
                 text_parts.at[rest, k, :, tail], came_y.at[3 - k], a_send.at[1, k - 1], a_recv.at[1, k - 1], along_y(k)
             )
         )
-    gifts = give(1, take(0, gifts))
 
     text_share.wait_recv()
     for half in (0, 1):
@@ -279,7 +290,7 @@
                 along_x(k),
             )
         )
-    gifts = give(2, take(1, gifts))
+    gifts = give(1, take(0, gifts))
 
     arrived(to_z)
     total = text_near[...]
@@ -300,7 +311,7 @@
         out_z.append(
             copy(text_parts.at[k, 0], last_z.at[3 - k], b_send.at[1, k - 1], b_recv.at[1, k - 1], along_z(k))
         )
-    gifts = give(3, take(2, gifts))
+    gifts = give(2, take(1, gifts))
     arrived(to_x)
     total = image_own[...]
     for k in range(3):
@@ -317,7 +328,6 @@
                 in_block(k),
             )
         )
-    gifts = give(4, take(3, gifts))
     arrived(out_block)
     total = image_own[0:ROWS]
     for k in range(3):
@@ -328,7 +338,7 @@
     for k in range(3):
         total = total + last_y[k].astype(F32) + last_z[k].astype(F32)
     text_grad_ref[...] = total
-    loss_ref[0] = jnp.sum(take(4, gifts)) / 8192.0
+    loss_ref[...] = jnp.full(loss_ref.shape, jnp.sum(take(2, gifts)) / 8192.0, F32)
     for made in sent:
         made.wait_send()
 
@@ -336,15 +346,14 @@
 def local(image_embed, text_embed, logit_scale, logit_bias):
     width = image_embed.shape[1]
     vmem = pl.BlockSpec(memory_space=pltpu.VMEM)
-    smem = pl.BlockSpec(memory_space=pltpu.SMEM)
     hbm = pl.BlockSpec(memory_space=pltpu.HBM)
     dma = pltpu.SemaphoreType.DMA
     grad = jax.ShapeDtypeStruct((ROWS, width), F32)
-    return pl.pallas_call(
+    loss, image_grad, text_grad = pl.pallas_call(
         kernel,
-        out_shape=(jax.ShapeDtypeStruct((1,), F32), grad, grad),
-        in_specs=[hbm, hbm, smem, smem],
-        out_specs=(smem, vmem, vmem),
+        out_shape=(jax.ShapeDtypeStruct((8, 128), F32), grad, grad),
+        in_specs=[hbm, hbm, hbm, hbm],
+        out_specs=(vmem, vmem, vmem),
         scratch_shapes=[
             pltpu.VMEM((2 * SET, width), BF16),
             pltpu.VMEM((2, 4, 4, ROWS, width), BF16),
@@ -362,8 +371,9 @@
             pltpu.VMEM((3, 4 * ROWS, width), BF16),
             pltpu.VMEM((3 * ROWS, width), BF16),
             pltpu.VMEM((3, ROWS, width), BF16),
-            pltpu.VMEM((5, 4, 8, 128), F32),
-            dma((2,)),
+            pltpu.VMEM((3, 8, 8, 128), F32),
+            pltpu.SMEM((2, 1), F32),
+            dma((4,)),
             dma((2, 3)),
             dma((2, 3)),
             dma((2, 3)),
@@ -380,14 +390,16 @@
             dma((3,)),
             dma((3,)),
             dma((3,)),
-            dma((5, 3)),
-            dma((5, 3)),
+            dma((3, 7)),
+            dma((3, 7)),
         ],
         compiler_params=pltpu.CompilerParams(
-            collective_id=0, has_side_effects=True, vmem_limit_bytes=60 * 2**20
+            collective_id=0, has_side_effects=True, vmem_limit_bytes=48 * 2**20
         ),
         name="pairs",
-    )(image_embed, text_embed, logit_scale, logit_bias)
+    )(*(pltpu.with_memory_space_constraint(a, pltpu.HBM) for a in (image_embed, text_embed)), logit_scale, logit_bias)
+
+    return loss[0, 0:1], image_grad, text_grad
 
 
 def solution(mesh):

time: 59.3 us -> 51.9 us (0.88)
  Pallas kernels: 53 us -> 48 us
  between operations: 3.69 us -> 1.93 us
    pallas_call x1, Pallas kernels: 53 us -> 48 us  [local(): pl.pallas_call(kernel, out_shape=(jax.ShapeDtypeStruct((8, 128), F32), gr...]
    unnamed x4 -> x2, local copies, waits for them, and re-layouts: 2.19 us -> 1.26 us
where the time goes in v3:
time: 51.9 us; the launch traced here: 51.7 us
  Pallas kernels  48 us (92%)
  between operations  1.93 us (4%)
  local copies, waits for them, and re-layouts  1.78 us (3%)
    pallas_call x1, Pallas kernels, local(): pl.pallas_call(kernel, out_shape=(jax.ShapeDtypeStruct((8, 128), F32), gr...  48 us
    unnamed x2, local copies, waits for them, and re-layouts  1.26 us

profile of v3, /device:TPU:1, one launch (start us, length us, event | category | flops | bytes accessed | tf_op | source)
XLA Modules:
  0.0 51.7 jit_solution(2403210684070980211)
XLA Ops:
  1.9 48.0 %pairs.1 = (f32[8,128]{1,0:T(8,128)S(1)}, f32[16,1152]{1,0:T(8,128)S(1)}, f32[16,1152]{1,0:T(8,128)S(1)}) custom-call(bf16[16,1152]{1,0:T(8,128)(2,1)} %image_ref.1, bf16[16,1152]{1,0:T(8,128)(2,1)} %text_ref.1, f32[1]{0:T(128)S(6)} %copy.9.scale_ref, f32[1]{0:T(128)S(6)} %copy.10.bias_ref), custom_call_target="tpu_custom_call" | custom-call | tf_op jit(solution)/shard_map/pairs/pallas_call | solution.py:352
  49.9 0.5 slice.3
  50.4 0.6 %copy.11 = f32[16,1152]{1,0:T(8,128)} copy(f32[16,1152]{1,0:T(8,128)S(1)} %get-tuple-element.13) | data formatting | bytes 147456
  51.1 0.6 %copy.12 = f32[16,1152]{1,0:T(8,128)} copy(f32[16,1152]{1,0:T(8,128)S(1)} %get-tuple-element.14) | data formatting | bytes 147456

commit v4 on v3

v4 whole, which is shorter than its diff:
```python
import jax
import jax.numpy as jnp
from jax import lax
from jax.experimental import pallas as pl
from jax.experimental.pallas import tpu as pltpu
from jax.sharding import PartitionSpec as P

MESH = pl.DeviceIdType.MESH
F32 = jnp.float32
BF16 = jnp.bfloat16
ROWS = 16
SET = 16 * ROWS
CUT = 640
NT = (((1,), (1,)), ((), ()))


def place():
    wide = lax.axis_index("wide")
    narrow = lax.axis_index("narrow")
    y = lax.rem(lax.div(wide, 2), 8)
    z = lax.div(wide, 16) * 4 + lax.rem(narrow, 4)
    return lax.div(narrow, 4), y, z, lax.rem(wide, 2)


def device(x, y, z, core):
    return (lax.div(z, 4) * 16 + y * 2 + core, x * 4 + lax.rem(z, 4))


def pair_weights(dots, scaling, offset, diagonal):
    logits = scaling * dots + offset
    if diagonal is None:
        turned = logits
    else:
        turned = jnp.where(diagonal, -logits, logits)
    small = jnp.exp(-jnp.abs(turned))
    chance = jnp.where(turned >= 0.0, 1.0, small) / (1.0 + small)
    weights = scaling * chance
    if diagonal is not None:
        weights = jnp.where(diagonal, -weights, weights)
    return turned, small, weights.astype(BF16)


def kernel(
    image_ref,
    text_ref,
    scale_ref,
    bias_ref,
    loss_ref,
    image_grad_ref,
    text_grad_ref,
    images,
    texts,
    weights,
    text_parts,
    text_near,
    text_far,
    text_own,
    came_z,
    came_y,
    last_y,
    last_z,
    image_parts,
    image_own,
    came_x,
    block_parts,
    last_block,
    totals,
    numbers,
    load,
    send,
    recv,
):
    x, y, z, core = place()
    steps = (2, 1, 3)
    flipped_y = y + 1 - 2 * lax.rem(y, 2)
    flipped_z = z + 1 - 2 * lax.rem(z, 2)
    all_steps = (4, 3, 5, 2, 6, 1, 7)

    def along_x(k):
        return device(lax.rem(x + k, 4), y, z, core)

    def ring_y(k):
        return device(x, lax.rem(y + k, 8), z, core)

    def ring_z(k):
        return device(x, y, lax.rem(z + k, 8), core)

    def along_y(k):
        return ring_y(2 * k)

    def along_z(k):
        return ring_z(2 * k)

    def in_row(k):
        return device(lax.rem(x + k // 2, 4), y, z, 1 - core if k % 2 else core)

    def in_block(k):
        return device(x, flipped_y if k % 2 else y, flipped_z if k // 2 else z, core)

    barrier = pltpu.get_barrier_semaphore()
    for reach in (ring_y, ring_z, in_row):
        for k in all_steps:
            pl.semaphore_signal(barrier, inc=1, device_id=reach(k), device_id_type=MESH)
    pl.semaphore_signal(barrier, inc=1, device_id=in_block(3), device_id_type=MESH)
    loads = [
        pltpu.make_async_copy(image_ref, images.at[pl.ds(0, ROWS)], load.at[0]),
        pltpu.make_async_copy(text_ref, texts.at[0, 0, 0], load.at[1]),
        pltpu.make_async_copy(scale_ref, numbers.at[0], load.at[2]),
        pltpu.make_async_copy(bias_ref, numbers.at[1], load.at[3]),
    ]
    for made in loads:
        made.start()
    for made in loads:
        made.wait()
    scaling = numbers[0, 0]
    offset = numbers[1, 0]
    pl.semaphore_wait(barrier, 22)

    groups = []

    def start(whole, copies):
        group = len(groups)
        groups.append(whole)
        for src, dst, to in copies:
            pltpu.make_async_remote_copy(
                src_ref=src,
                dst_ref=dst,
                send_sem=send.at[group],
                recv_sem=recv.at[group],
                device_id=to,
                device_id_type=MESH,
            ).start()
        return group

    def arrived(*which):
        for group in which:
            pltpu.make_async_copy(groups[group], groups[group], recv.at[group]).wait()

    rest = pl.ds(1, 3)
    head, tail = pl.ds(0, CUT), pl.ds(CUT, texts.shape[-1] - CUT)
    bundle = 4 * ROWS
    own = images.at[pl.ds(0, ROWS)]
    from_block = start(
        images.at[pl.ds(ROWS, 3 * ROWS)],
        [(own, images.at[pl.ds(k * ROWS, ROWS)], in_block(k)) for k in (3, 1, 2)],
    )

    def own_text(part, reach, along_near):
        src = texts.at[0, 0, 0, :, part]
        whole = texts.at[0, 0, rest, :, part] if along_near else texts.at[0, rest, 0, :, part]
        return start(
            whole,
            [
                (src, texts.at[0, 0, 4 - k, :, part] if along_near else texts.at[0, 4 - k, 0, :, part], reach(k))
                for k in steps
            ],
        )

    head_y = own_text(head, along_y, True)
    tail_z = own_text(tail, along_z, False)
    tail_y = own_text(tail, along_y, True)
    head_z = own_text(head, along_z, False)
    arrived(from_block)
    from_x = start(
        images.at[pl.ds(bundle, 3 * bundle)],
        [
            (images.at[pl.ds(0, bundle)], images.at[pl.ds((4 - k) * bundle, bundle)], along_x(k))
            for k in steps
        ],
    )
    arrived(head_y)
    passed_z = start(
        texts.at[0, rest, rest, :, head],
        [(texts.at[0, 0, rest, :, head], texts.at[0, 4 - k, rest, :, head], along_z(k)) for k in steps],
    )
    arrived(tail_z)
    passed_y = start(
        texts.at[0, rest, rest, :, tail],
        [(texts.at[0, rest, 0, :, tail], texts.at[0, rest, 4 - k, :, tail], along_y(k)) for k in steps],
    )
    arrived(from_x)
    image_share = start(
        images.at[pl.ds(SET, SET)], [(images.at[pl.ds(0, SET)], images.at[pl.ds(SET, SET)], in_row(1))]
    )
    arrived(tail_y, head_z, passed_z, passed_y)
    text_share = start(texts.at[1], [(texts.at[0], texts.at[1], in_row(1))])

    rows = lax.broadcasted_iota(jnp.int32, (SET, SET), 0)
    columns = lax.broadcasted_iota(jnp.int32, (SET, SET), 1)
    diagonal = (rows == columns) & (rows < ROWS)

    stages = ((y, ring_y), (z, ring_z), (2 * x + core, in_row))

    def give(stage, value):
        slot, reach = stages[stage]
        totals[stage, slot] = value
        mine = totals.at[stage, slot]
        return start(totals.at[stage, pl.ds(0, 7)], [(mine, mine, reach(k)) for k in all_steps])

    def take(stage, gifts):
        arrived(gifts)
        value = totals[stage, 0]
        for k in range(1, 8):
            value = value + totals[stage, k]
        return value

    def text_set(half):
        return texts[half].reshape(SET, texts.shape[-1])

    loss = jnp.zeros((8, 128), F32)
    for half in (0, 1):
        if half == 1:
            arrived(image_share)
        dots = lax.dot_general(
            text_set(0), images[half * SET : (half + 1) * SET], NT, preferred_element_type=F32
        )
        turned, small, tile = pair_weights(dots, scaling, offset, diagonal if half == 0 else None)
        weights[:, half * SET : (half + 1) * SET] = tile
        terms = jnp.maximum(turned, 0.0) + jnp.log1p(small)
        terms = jnp.sum(terms.reshape(SET // 8, 8, SET), axis=0)
        loss = loss + terms[:, 0:128] + terms[:, 128:256]
    gifts = give(0, loss)
    grads = jnp.dot(weights[...], images[...], preferred_element_type=F32).reshape(4, 4, ROWS, -1)
    text_parts[...] = grads.astype(BF16)
    text_near[...] = grads[0, 1:4, :, 0:CUT]
    text_far[...] = grads[1:4, 0, :, CUT:]
    text_own[...] = grads[0, 0]
    to_z = start(came_z, [(text_parts.at[k, rest, :, head], came_z.at[3 - k], along_z(k)) for k in steps])
    to_y = start(came_y, [(text_parts.at[rest, k, :, tail], came_y.at[3 - k], along_y(k)) for k in steps])

    arrived(text_share)
    for half in (0, 1):
        dots = lax.dot_general(images[0:SET], text_set(half), NT, preferred_element_type=F32)
        weights[:, half * SET : (half + 1) * SET] = pair_weights(
            dots, scaling, offset, diagonal if half == 0 else None
        )[2]
    grads = jnp.dot(
        weights[...], texts[...].reshape(2 * SET, texts.shape[-1]), preferred_element_type=F32
    )
    image_own[...] = grads[0:bundle]
    image_parts[...] = grads[bundle:].astype(BF16)
    to_x = start(
        came_x,
        [(image_parts.at[pl.ds((k - 1) * bundle, bundle)], came_x.at[3 - k], along_x(k)) for k in steps],
    )
    gifts = give(1, take(0, gifts))

    arrived(to_z)
    total = text_near[...]
    for k in range(3):
        total = total + came_z[k].astype(F32)
    text_parts[0, 1:4, :, 0:CUT] = total.astype(BF16)
    out_y = start(last_y, [(text_parts.at[0, k], last_y.at[3 - k], along_y(k)) for k in steps])
    arrived(to_y)
    total = text_far[...]
    for k in range(3):
        total = total + came_y[k].astype(F32)
    text_parts[1:4, 0, :, CUT:] = total.astype(BF16)
    out_z = start(last_z, [(text_parts.at[k, 0], last_z.at[3 - k], along_z(k)) for k in steps])
    arrived(to_x)
    total = image_own[...]
    for k in range(3):
        total = total + came_x[k].astype(F32)
    image_own[0:ROWS] = total[0:ROWS]
    block_parts[...] = total[ROWS:].astype(BF16)
    out_block = start(
        last_block,
        [
            (block_parts.at[pl.ds((k - 1) * ROWS, ROWS)], last_block.at[k - 1], in_block(k))
            for k in (3, 1, 2)
        ],
    )
    gifts = give(2, take(1, gifts))
    arrived(out_y, out_z)
    total = text_own[...]
    for k in range(3):
        total = total + last_y[k].astype(F32) + last_z[k].astype(F32)
    text_grad_ref[...] = total
    arrived(out_block)
    total = image_own[0:ROWS]
    for k in range(3):
        total = total + last_block[k].astype(F32)
    image_grad_ref[...] = total
    loss_ref[...] = jnp.full(loss_ref.shape, jnp.sum(take(2, gifts)) / 8192.0, F32)
    for group, whole in enumerate(groups):
        pltpu.make_async_copy(whole, whole, send.at[group]).wait()


def finish(loss_ref, image_ref, text_ref, loss_out, image_out, text_out, sems):
    copies = [
        pltpu.make_async_copy(image_ref, image_out, sems.at[0]),
        pltpu.make_async_copy(text_ref, text_out, sems.at[1]),
        pltpu.make_async_copy(loss_ref.at[pl.ds(0, 1)], loss_out, sems.at[2]),
    ]
    for made in copies:
        made.start()
    for made in copies:
        made.wait()


def local(image_embed, text_embed, logit_scale, logit_bias):
    width = image_embed.shape[1]
    vmem = pl.BlockSpec(memory_space=pltpu.VMEM)
    hbm = pl.BlockSpec(memory_space=pltpu.HBM)
    dma = pltpu.SemaphoreType.DMA
    grad = jax.ShapeDtypeStruct((ROWS, width), F32)
    loss, image_grad, text_grad = pl.pallas_call(
        kernel,
        out_shape=(jax.ShapeDtypeStruct((8, 128), F32), grad, grad),
        in_specs=[hbm, hbm, hbm, hbm],
        out_specs=(vmem, vmem, vmem),
        scratch_shapes=[
            pltpu.VMEM((2 * SET, width), BF16),
            pltpu.VMEM((2, 4, 4, ROWS, width), BF16),
            pltpu.VMEM((SET, 2 * SET), BF16),
            pltpu.VMEM((4, 4, ROWS, width), BF16),
            pltpu.VMEM((3, ROWS, CUT), F32),
            pltpu.VMEM((3, ROWS, width - CUT), F32),
            pltpu.VMEM((ROWS, width), F32),
            pltpu.VMEM((3, 3, ROWS, CUT), BF16),
            pltpu.VMEM((3, 3, ROWS, width - CUT), BF16),
            pltpu.VMEM((3, ROWS, width), BF16),
            pltpu.VMEM((3, ROWS, width), BF16),
            pltpu.VMEM((12 * ROWS, width), BF16),
            pltpu.VMEM((4 * ROWS, width), F32),
            pltpu.VMEM((3, 4 * ROWS, width), BF16),
            pltpu.VMEM((3 * ROWS, width), BF16),
            pltpu.VMEM((3, ROWS, width), BF16),
            pltpu.VMEM((3, 8, 8, 128), F32),
            pltpu.SMEM((2, 1), F32),
            dma((4,)),
            dma((19,)),
            dma((19,)),
        ],
        compiler_params=pltpu.CompilerParams(
            collective_id=0, has_side_effects=True, vmem_limit_bytes=48 * 2**20
        ),
        name="pairs",
    )(
        pltpu.with_memory_space_constraint(image_embed, pltpu.HBM),
        pltpu.with_memory_space_constraint(text_embed, pltpu.HBM),
        logit_scale,
        logit_bias,
    )
    loss, image_grad, text_grad = pl.pallas_call(
        finish,
        out_shape=(jax.ShapeDtypeStruct((1, 128), F32), grad, grad),
        in_specs=[vmem, vmem, vmem],
        out_specs=(hbm, hbm, hbm),
        scratch_shapes=[dma((3,))],
        compiler_params=pltpu.CompilerParams(vmem_limit_bytes=2**20),
        name="finish",
    )(loss, image_grad, text_grad)
    return loss[0, 0:1], image_grad, text_grad


def solution(mesh):
    rows = P(("wide", "narrow"), None)
    return jax.shard_map(
        local, mesh=mesh, in_specs=(rows, rows, P(), P()), out_specs=(P(), rows, rows), check_vma=False
    )
```

time: 51.9 us -> 49.3 us (0.950)
  local copies, waits for them, and re-layouts: 1.78 us -> 0 us
  Pallas kernels: 48 us -> 47.2 us
    pallas_call x1, Pallas kernels: 48 us -> 46.5 us  [local(): pl.pallas_call(kernel, out_shape=(jax.ShapeDtypeStruct((8, 128), F32), gr...]
    unnamed x2 -> x0, local copies, waits for them, and re-layouts: 1.26 us -> none
    pallas_call x0 -> x1, Pallas kernels: none -> 0.69 us  [local(): pl.pallas_call(finish, out_shape=(jax.ShapeDtypeStruct((1, 128), F32), gr...]
where the time goes in v4:
time: 49.3 us; the launch traced here: 49.1 us
  Pallas kernels  47.2 us (96%)
  between operations  1.93 us (4%)
    pallas_call x1, Pallas kernels, local(): pl.pallas_call(kernel, out_shape=(jax.ShapeDtypeStruct((8, 128), F32), gr...  46.5 us

profile of v4, /device:TPU:1, one launch (start us, length us, event | category | flops | bytes accessed | tf_op | source)
XLA Modules:
  0.0 49.1 jit_solution(9726361933407770620)
XLA Ops:
  1.9 46.5 %pairs.1 = (f32[8,128]{1,0:T(8,128)S(1)}, f32[16,1152]{1,0:T(8,128)S(1)}, f32[16,1152]{1,0:T(8,128)S(1)}) custom-call(bf16[16,1152]{1,0:T(8,128)(2,1)} %image_ref.1, bf16[16,1152]{1,0:T(8,128)(2,1)} %text_ref.1, f32[1]{0:T(128)S(6)} %copy.7.scale_ref, f32[1]{0:T(128)S(6)} %copy.8.bias_ref), custom_call_target="tpu_custom_call" | custom-call | tf_op jit(solution)/shard_map/pairs/pallas_call | solution.py:307
  48.4 0.7 %finish.1 = (f32[1,128]{1,0:T(1,128)}, f32[16,1152]{1,0:T(8,128)}, f32[16,1152]{1,0:T(8,128)}) custom-call(f32[8,128]{1,0:T(8,128)S(1)} %get-tuple-element.9.loss_ref, f32[16,1152]{1,0:T(8,128)S(1)} %get-tuple-element.10.image_ref, f32[16,1152]{1,0:T(8,128)S(1)} %get-tuple-element.11.text_ref), custom_call_target="tpu_custom_call" | custom-call | tf_op jit(solution)/shard_map/finish/pallas_call | solution.py:345

commit v5 on v4

v5 whole, which is shorter than its diff:
```python
import jax
import jax.numpy as jnp
from jax import lax
from jax.experimental import pallas as pl
from jax.experimental.pallas import tpu as pltpu
from jax.sharding import PartitionSpec as P

MESH = pl.DeviceIdType.MESH
F32 = jnp.float32
BF16 = jnp.bfloat16
ROWS = 16
SET = 16 * ROWS
CUT = 640
SLOT = {1: 1, 3: 2, 2: 3}
NT = (((1,), (1,)), ((), ()))


def place():
    wide = lax.axis_index("wide")
    narrow = lax.axis_index("narrow")
    y = lax.rem(lax.div(wide, 2), 8)
    z = lax.div(wide, 16) * 4 + lax.rem(narrow, 4)
    return lax.div(narrow, 4), y, z, lax.rem(wide, 2)


def device(x, y, z, core):
    return (lax.div(z, 4) * 16 + y * 2 + core, x * 4 + lax.rem(z, 4))


def turned_logits(dots, scaling, offset, diagonal):
    logits = scaling * dots + offset
    return logits if diagonal is None else jnp.where(diagonal, -logits, logits)


def pair_weights(turned, scaling, diagonal):
    small = jnp.exp(-jnp.abs(turned))
    weights = scaling * (jnp.where(turned >= 0.0, 1.0, small) / (1.0 + small))
    if diagonal is not None:
        weights = jnp.where(diagonal, -weights, weights)
    return weights.astype(BF16)


def pair_loss(turned):
    terms = jnp.maximum(turned, 0.0) + jnp.log1p(jnp.exp(-jnp.abs(turned)))
    terms = jnp.sum(terms.reshape(-1, 8, terms.shape[-1]), axis=0)
    return sum(terms[:, k : k + 128] for k in range(0, terms.shape[-1], 128))


def kernel(
    image_ref,
    text_ref,
    scale_ref,
    bias_ref,
    loss_ref,
    image_grad_ref,
    text_grad_ref,
    images,
    texts,
    weights,
    kept,
    text_parts,
    text_near,
    text_far,
    text_own,
    came_z,
    came_y,
    last_y,
    last_z,
    image_parts,
    image_own,
    came_x,
    came_last,
    block_parts,
    last_block,
    totals,
    numbers,
    load,
    send,
    recv,
    shared_loss,
    hop,
    loss_send,
    loss_recv,
):
    x, y, z, core = place()
    steps = (2, 1, 3)
    flipped_y = y + 1 - 2 * lax.rem(y, 2)
    flipped_z = z + 1 - 2 * lax.rem(z, 2)
    all_steps = (4, 3, 5, 2, 6, 1, 7)

    def along_x(k):
        return device(lax.rem(x + k, 4), y, z, core)

    def ring_y(k):
        return device(x, lax.rem(y + k, 8), z, core)

    def ring_z(k):
        return device(x, y, lax.rem(z + k, 8), core)

    def along_y(k):
        return ring_y(2 * k)

    def along_z(k):
        return ring_z(2 * k)

    def in_block(k):
        return device(x, flipped_y if k % 2 else y, flipped_z if k // 2 else z, core)

    sibling = device(x, y, z, 1 - core)

    barrier = pltpu.get_barrier_semaphore()
    for reach in (ring_y, ring_z):
        for k in all_steps:
            pl.semaphore_signal(barrier, inc=1, device_id=reach(k), device_id_type=MESH)
    for to in (along_x(2), along_x(1), along_x(3), in_block(3), sibling):
        pl.semaphore_signal(barrier, inc=1, device_id=to, device_id_type=MESH)
    loads = [
        pltpu.make_async_copy(image_ref, images.at[pl.ds(0, ROWS)], load.at[0]),
        pltpu.make_async_copy(text_ref, texts.at[0, 0, 0], load.at[1]),
        pltpu.make_async_copy(scale_ref, numbers.at[0], load.at[2]),
        pltpu.make_async_copy(bias_ref, numbers.at[1], load.at[3]),
    ]
    for made in loads:
        made.start()
    pl.semaphore_wait(barrier, 19)

    groups = []

    def start(whole, copies, group=None):
        if group is None:
            group = len(groups)
            groups.append(whole)
        for src, dst, to in copies:
            pltpu.make_async_remote_copy(
                src_ref=src,
                dst_ref=dst,
                send_sem=send.at[group],
                recv_sem=recv.at[group],
                device_id=to,
                device_id_type=MESH,
            ).start()
        return group

    def arrived(*which):
        for group in which:
            pltpu.make_async_copy(groups[group], groups[group], recv.at[group]).wait()

    width = texts.shape[-1]
    first, near, far, rest = pl.ds(0, 1), pl.ds(1, 2), pl.ds(3, 1), pl.ds(1, 3)
    head, tail = pl.ds(0, CUT), pl.ds(CUT, width - CUT)
    bundle = 4 * ROWS

    def own_text(part, reach, along_near, ways):
        def there(slots):
            return texts.at[0, first, slots, :, part] if along_near else texts.at[0, slots, first, :, part]

        def slot(k):
            at = SLOT[4 - k]
            return texts.at[0, 0, at, :, part] if along_near else texts.at[0, at, 0, :, part]

        slots = rest if len(ways) == 3 else (far if ways == (2,) else near)
        return start(there(slots), [(text_ref.at[:, part], slot(k), reach(k)) for k in ways])

    from_block = start(
        images.at[pl.ds(ROWS, 3 * ROWS)],
        [(image_ref, images.at[pl.ds(k * ROWS, ROWS)], in_block(k)) for k in (3, 1, 2)],
    )
    head_y_far = own_text(head, along_y, True, (2,))
    tail_z_far = own_text(tail, along_z, False, (2,))
    head_y = own_text(head, along_y, True, (1, 3))
    tail_z = own_text(tail, along_z, False, (1, 3))
    own_x = start(
        images.at[pl.ds(0, 3 * ROWS)],
        [(image_ref, images.at[pl.ds((4 - k) * bundle, ROWS)], along_x(k)) for k in steps],
    )
    tail_y = own_text(tail, along_y, True, steps)
    head_z = own_text(head, along_z, False, steps)

    def pass_z(slots, group=None):
        return start(
            texts.at[0, rest, rest, :, head],
            [(texts.at[0, 0, slots, :, head], texts.at[0, SLOT[4 - k], slots, :, head], along_z(k)) for k in steps],
            group,
        )

    def pass_y(slots, group=None):
        return start(
            texts.at[0, rest, rest, :, tail],
            [(texts.at[0, slots, 0, :, tail], texts.at[0, slots, SLOT[4 - k], :, tail], along_y(k)) for k in steps],
            group,
        )

    arrived(from_block)
    block = pl.ds(ROWS, 3 * ROWS)
    from_x = start(
        images.at[pl.ds(0, 9 * ROWS)],
        [
            (images.at[block], images.at[pl.ds((4 - k) * bundle + ROWS, 3 * ROWS)], along_x(k))
            for k in steps
        ],
    )
    arrived(head_y)
    passed_z = pass_z(near)
    arrived(tail_z)
    passed_y = pass_y(near)
    arrived(head_y_far)
    pass_z(far, passed_z)
    arrived(tail_z_far)
    pass_y(far, passed_y)
    for made in loads:
        made.wait()
    scaling = numbers[0, 0]
    offset = numbers[1, 0]
    arrived(own_x, from_x)
    image_share = start(
        images.at[pl.ds(SET, SET)], [(images.at[pl.ds(0, SET)], images.at[pl.ds(SET, SET)], sibling)]
    )
    arrived(tail_y, head_z, passed_z, passed_y)
    text_share = start(texts.at[1], [(texts.at[0], texts.at[1], sibling)])

    rows = lax.broadcasted_iota(jnp.int32, (SET, SET), 0)
    columns = lax.broadcasted_iota(jnp.int32, (SET, SET), 1)
    diagonal = (rows == columns) & (rows < ROWS)

    stages = ((y, ring_y, all_steps), (z, ring_z, all_steps), (x, along_x, steps))

    def across(src, dst, at):
        return pltpu.make_async_remote_copy(
            src_ref=src, dst_ref=dst, send_sem=hop.at[at], recv_sem=hop.at[at + 1], device_id=sibling, device_id_type=MESH
        )

    def ring(stage):
        slot, reach, ways = stages[stage]
        mine = totals.at[stage, slot]
        return [
            pltpu.make_async_remote_copy(
                src_ref=mine,
                dst_ref=mine,
                send_sem=loss_send.at[stage],
                recv_sem=loss_recv.at[stage],
                device_id=reach(k),
                device_id_type=MESH,
            )
            for k in ways
        ], totals.at[stage, pl.ds(0, len(ways))]

    def give(stage, value):
        totals[stage, stages[stage][0]] = value
        for made in ring(stage)[0]:
            made.start()

    def take(stage):
        whole = ring(stage)[1]
        pltpu.make_async_copy(whole, whole, loss_recv.at[stage]).wait()
        value = totals[stage, 0]
        for k in range(1, len(stages[stage][2]) + 1):
            value = value + totals[stage, k]
        return value

    def on_core_1(action):
        pl.when(core == 1)(action)

    def on_core_0(action):
        pl.when(core == 0)(action)

    def loss_start(value):
        shared_loss[0] = value
        on_core_0(across(shared_loss.at[0], shared_loss.at[1], 0).start)

    def loss_y():
        across(shared_loss.at[0], shared_loss.at[1], 0).wait_recv()
        give(0, shared_loss[0] + shared_loss[1])

    def loss_end():
        shared_loss[2] = take(2)
        across(shared_loss.at[2], shared_loss.at[3], 2).start()
        loss_ref[...] = jnp.full(loss_ref.shape, jnp.sum(shared_loss[2]) / 8192.0, F32)
        across(shared_loss.at[2], shared_loss.at[3], 2).wait_send()
        for stage in range(3):
            whole = ring(stage)[1]
            pltpu.make_async_copy(whole, whole, loss_send.at[stage]).wait()

    def loss_got():
        across(shared_loss.at[2], shared_loss.at[3], 2).wait_recv()
        loss_ref[...] = jnp.full(loss_ref.shape, jnp.sum(shared_loss[3]) / 8192.0, F32)
        across(shared_loss.at[0], shared_loss.at[1], 0).wait_send()

    def text_set(half):
        return texts[half].reshape(SET, width)

    for half in (0, 1):
        if half == 1:
            arrived(image_share)
        part = slice(half * SET, (half + 1) * SET)
        mask = diagonal if half == 0 else None
        dots = lax.dot_general(text_set(0), images[part], NT, preferred_element_type=F32)
        turned = turned_logits(dots, scaling, offset, mask)
        kept[:, part] = turned
        weights[:, part] = pair_weights(turned, scaling, mask)
    loss_start(pair_loss(kept[...]))
    grads = jnp.dot(weights[...], images[...], preferred_element_type=F32).reshape(4, 4, ROWS, -1)
    text_parts[...] = grads.astype(BF16)
    text_near[...] = grads[0, 1:4, :, 0:CUT]
    text_far[...] = grads[1:4, 0, :, CUT:]
    text_own[...] = grads[0, 0]

    def to_z(there, here):
        return start(
            came_z.at[:, there],
            [(text_parts.at[SLOT[k], here, :, head], came_z.at[SLOT[4 - k] - 1, there], along_z(k)) for k in steps],
        )

    def to_y(there, here):
        return start(
            came_y.at[:, there],
            [(text_parts.at[here, SLOT[k], :, tail], came_y.at[SLOT[4 - k] - 1, there], along_y(k)) for k in steps],
        )

    to_z_far, to_y_far = to_z(pl.ds(2, 1), far), to_y(pl.ds(2, 1), far)
    to_z_near, to_y_near = to_z(pl.ds(0, 2), near), to_y(pl.ds(0, 2), near)

    on_core_1(loss_y)

    arrived(text_share)
    for half in (0, 1):
        dots = lax.dot_general(images[0:SET], text_set(half), NT, preferred_element_type=F32)
        mask = diagonal if half == 0 else None
        turned = turned_logits(dots, scaling, offset, mask)
        weights[:, half * SET : (half + 1) * SET] = pair_weights(turned, scaling, mask)
    grads = jnp.dot(weights[...], texts[...].reshape(2 * SET, width), preferred_element_type=F32)
    image_own[...] = grads[0:bundle]
    image_parts[...] = grads[bundle:].astype(BF16)
    to_x = start(
        came_x,
        [
            (image_parts.at[pl.ds((k - 1) * bundle + ROWS, 3 * ROWS)], came_x.at[3 - k], along_x(k))
            for k in steps
        ],
    )
    on_core_1(lambda: give(1, take(0)))
    def out_y(slots, ways):
        for at in slots:
            total = text_near[at - 1]
            for k in range(3):
                total = total + came_z[k, at - 1].astype(F32)
            text_parts[0, at, :, 0:CUT] = total.astype(BF16)
        return start(
            last_y.at[pl.ds(slots[0] - 1, len(slots)), :, head],
            [(text_parts.at[0, SLOT[k], :, head], last_y.at[SLOT[4 - k] - 1, :, head], along_y(k)) for k in ways],
        )

    def out_z(slots, ways):
        for at in slots:
            total = text_far[at - 1]
            for k in range(3):
                total = total + came_y[k, at - 1].astype(F32)
            text_parts[at, 0, :, CUT:] = total.astype(BF16)
        return start(
            last_z.at[pl.ds(slots[0] - 1, len(slots)), :, tail],
            [(text_parts.at[SLOT[k], 0, :, tail], last_z.at[SLOT[4 - k] - 1, :, tail], along_z(k)) for k in ways],
        )

    arrived(to_z_far)
    outs = [out_y((3,), (2,))]
    arrived(to_y_far)
    outs.append(out_z((3,), (2,)))
    last_x = start(
        came_last,
        [(image_parts.at[pl.ds((k - 1) * bundle, ROWS)], came_last.at[3 - k], along_x(k)) for k in steps],
    )
    direct_y = start(
        last_y.at[:, :, tail],
        [(text_parts.at[0, SLOT[k], :, tail], last_y.at[SLOT[4 - k] - 1, :, tail], along_y(k)) for k in steps],
    )
    direct_z = start(
        last_z.at[:, :, head],
        [(text_parts.at[SLOT[k], 0, :, head], last_z.at[SLOT[4 - k] - 1, :, head], along_z(k)) for k in steps],
    )
    arrived(to_z_near)
    outs.append(out_y((1, 2), (1, 3)))
    arrived(to_y_near)
    outs.append(out_z((1, 2), (1, 3)))
    arrived(to_x)
    total = image_own[ROWS:]
    for k in range(3):
        total = total + came_x[k].astype(F32)
    block_parts[...] = total.astype(BF16)
    out_block = start(
        last_block,
        [
            (block_parts.at[pl.ds((k - 1) * ROWS, ROWS)], last_block.at[k - 1], in_block(k))
            for k in (3, 1, 2)
        ],
    )
    on_core_1(lambda: give(2, take(1)))
    arrived(direct_y, direct_z, *outs)
    total = text_own[...]
    for k in range(3):
        total = total + last_y[k].astype(F32) + last_z[k].astype(F32)
    text_grad_ref[...] = total
    arrived(last_x, out_block)
    total = image_own[0:ROWS]
    for k in range(3):
        total = total + came_last[k].astype(F32) + last_block[k].astype(F32)
    image_grad_ref[...] = total
    on_core_1(loss_end)
    on_core_0(loss_got)
    for group, whole in enumerate(groups):
        pltpu.make_async_copy(whole, whole, send.at[group]).wait()


def finish(loss_ref, image_ref, text_ref, loss_out, image_out, text_out, sems):
    copies = [
        pltpu.make_async_copy(image_ref, image_out, sems.at[0]),
        pltpu.make_async_copy(text_ref, text_out, sems.at[1]),
        pltpu.make_async_copy(loss_ref.at[pl.ds(0, 1)], loss_out, sems.at[2]),
    ]
    for made in copies:
        made.start()
    for made in copies:
        made.wait()


def local(image_embed, text_embed, logit_scale, logit_bias):
    width = image_embed.shape[1]
    vmem = pl.BlockSpec(memory_space=pltpu.VMEM)
    hbm = pl.BlockSpec(memory_space=pltpu.HBM)
    dma = pltpu.SemaphoreType.DMA
    grad = jax.ShapeDtypeStruct((ROWS, width), F32)
    loss, image_grad, text_grad = pl.pallas_call(
        kernel,
        out_shape=(jax.ShapeDtypeStruct((8, 128), F32), grad, grad),
        in_specs=[hbm, hbm, hbm, hbm],
        out_specs=(vmem, vmem, vmem),
        scratch_shapes=[
            pltpu.VMEM((2 * SET, width), BF16),
            pltpu.VMEM((2, 4, 4, ROWS, width), BF16),
            pltpu.VMEM((SET, 2 * SET), BF16),
            pltpu.VMEM((SET, 2 * SET), F32),
            pltpu.VMEM((4, 4, ROWS, width), BF16),
            pltpu.VMEM((3, ROWS, CUT), F32),
            pltpu.VMEM((3, ROWS, width - CUT), F32),
            pltpu.VMEM((ROWS, width), F32),
            pltpu.VMEM((3, 3, ROWS, CUT), BF16),
            pltpu.VMEM((3, 3, ROWS, width - CUT), BF16),
            pltpu.VMEM((3, ROWS, width), BF16),
            pltpu.VMEM((3, ROWS, width), BF16),
            pltpu.VMEM((12 * ROWS, width), BF16),
            pltpu.VMEM((4 * ROWS, width), F32),
            pltpu.VMEM((3, 3 * ROWS, width), BF16),
            pltpu.VMEM((3, ROWS, width), BF16),
            pltpu.VMEM((3 * ROWS, width), BF16),
            pltpu.VMEM((3, ROWS, width), BF16),
            pltpu.VMEM((3, 8, 8, 128), F32),
            pltpu.SMEM((2, 1), F32),
            dma((4,)),
            dma((26,)),
            dma((26,)),
            pltpu.VMEM((4, 8, 128), F32),
            dma((4,)),
            dma((3,)),
            dma((3,)),
        ],
        compiler_params=pltpu.CompilerParams(
            collective_id=0, has_side_effects=True, vmem_limit_bytes=48 * 2**20
        ),
        name="pairs",
    )(
        pltpu.with_memory_space_constraint(image_embed, pltpu.HBM),
        pltpu.with_memory_space_constraint(text_embed, pltpu.HBM),
        logit_scale,
        logit_bias,
    )
    loss, image_grad, text_grad = pl.pallas_call(
        finish,
        out_shape=(jax.ShapeDtypeStruct((1, 128), F32), grad, grad),
        in_specs=[vmem, vmem, vmem],
        out_specs=(hbm, hbm, hbm),
        scratch_shapes=[dma((3,))],
        compiler_params=pltpu.CompilerParams(vmem_limit_bytes=2**20),
        name="finish",
    )(loss, image_grad, text_grad)
    return loss[0, 0:1], image_grad, text_grad


def solution(mesh):
    rows = P(("wide", "narrow"), None)
    return jax.shard_map(
        local, mesh=mesh, in_specs=(rows, rows, P(), P()), out_specs=(P(), rows, rows), check_vma=False
    )
```

time: 49.3 us -> 47.4 us (0.961)
  Pallas kernels: 47.2 us -> 45.1 us
    pallas_call x1, Pallas kernels: 46.5 us -> 44.4 us  [local(): pl.pallas_call(kernel, out_shape=(jax.ShapeDtypeStruct((8, 128), F32), gr...]
where the time goes in v5:
time: 47.4 us; the launch traced here: 47.1 us
  Pallas kernels  45.1 us (95%)
  between operations  1.93 us (4%)
    pallas_call x1, Pallas kernels, local(): pl.pallas_call(kernel, out_shape=(jax.ShapeDtypeStruct((8, 128), F32), gr...  44.4 us

profile of v5, /device:TPU:1, one launch (start us, length us, event | category | flops | bytes accessed | tf_op | source)
XLA Modules:
  0.0 47.1 jit_solution(15106046665836070031)
XLA Ops:
  1.9 44.4 %pairs.1 = (f32[8,128]{1,0:T(8,128)S(1)}, f32[16,1152]{1,0:T(8,128)S(1)}, f32[16,1152]{1,0:T(8,128)S(1)}) custom-call(bf16[16,1152]{1,0:T(8,128)(2,1)} %image_ref.1, bf16[16,1152]{1,0:T(8,128)(2,1)} %text_ref.1, f32[1]{0:T(128)S(6)} %copy.7.scale_ref, f32[1]{0:T(128)S(6)} %copy.8.bias_ref), custom_call_target="tpu_custom_call" | custom-call | tf_op jit(solution)/shard_map/pairs/pallas_call | solution.py:430
  46.4 0.7 %finish.1 = (f32[1,128]{1,0:T(1,128)}, f32[16,1152]{1,0:T(8,128)}, f32[16,1152]{1,0:T(8,128)}) custom-call(f32[8,128]{1,0:T(8,128)S(1)} %get-tuple-element.9.loss_ref, f32[16,1152]{1,0:T(8,128)S(1)} %get-tuple-element.10.image_ref, f32[16,1152]{1,0:T(8,128)S(1)} %get-tuple-element.11.text_ref), custom_call_target="tpu_custom_call" | custom-call | tf_op jit(solution)/shard_map/finish/pallas_call | solution.py:474

commit v6 on v5

--- a/solution.py
+++ b/solution.py
@@ -12,6 +12,8 @@
 SET = 16 * ROWS
 CUT = 640
 SLOT = {1: 1, 3: 2, 2: 3}
+GROUPS = 16
+SENT = (30 + 30 + 32) * ROWS
 NT = (((1,), (1,)), ((), ()))
 
 
@@ -64,15 +66,14 @@
     text_own,
     came_z,
     came_y,
-    last_y,
-    last_z,
+    last_text,
     image_parts,
     image_own,
     came_x,
-    came_last,
     block_parts,
-    last_block,
+    last_image,
     totals,
+    all_sent,
     numbers,
     load,
     send,
@@ -134,7 +135,7 @@
             pltpu.make_async_remote_copy(
                 src_ref=src,
                 dst_ref=dst,
-                send_sem=send.at[group],
+                send_sem=send,
                 recv_sem=recv.at[group],
                 device_id=to,
                 device_id_type=MESH,
@@ -150,7 +151,7 @@
     head, tail = pl.ds(0, CUT), pl.ds(CUT, width - CUT)
     bundle = 4 * ROWS
 
-    def own_text(part, reach, along_near, ways):
+    def own_text(part, reach, along_near, ways, group=None):
         def there(slots):
             return texts.at[0, first, slots, :, part] if along_near else texts.at[0, slots, first, :, part]
 
@@ -158,8 +159,9 @@
             at = SLOT[4 - k]
             return texts.at[0, 0, at, :, part] if along_near else texts.at[0, at, 0, :, part]
 
-        slots = rest if len(ways) == 3 else (far if ways == (2,) else near)
-        return start(there(slots), [(text_ref.at[:, part], slot(k), reach(k)) for k in ways])
+        return start(
+            there(far if ways == (2,) else near), [(text_ref.at[:, part], slot(k), reach(k)) for k in ways], group
+        )
 
     from_block = start(
         images.at[pl.ds(ROWS, 3 * ROWS)],
@@ -169,53 +171,55 @@
     tail_z_far = own_text(tail, along_z, False, (2,))
     head_y = own_text(head, along_y, True, (1, 3))
     tail_z = own_text(tail, along_z, False, (1, 3))
-    own_x = start(
-        images.at[pl.ds(0, 3 * ROWS)],
+    from_x = start(
+        images.at[pl.ds(bundle, 3 * bundle)],
         [(image_ref, images.at[pl.ds((4 - k) * bundle, ROWS)], along_x(k)) for k in steps],
     )
-    tail_y = own_text(tail, along_y, True, steps)
-    head_z = own_text(head, along_z, False, steps)
-
-    def pass_z(slots, group=None):
-        return start(
-            texts.at[0, rest, rest, :, head],
+    passed = start(texts.at[0, rest], [])
+    own_text(tail, along_y, True, steps, passed)
+    own_text(head, along_z, False, steps, passed)
+
+    def pass_z(slots):
+        start(
+            texts.at[0, rest],
             [(texts.at[0, 0, slots, :, head], texts.at[0, SLOT[4 - k], slots, :, head], along_z(k)) for k in steps],
-            group,
-        )
-
-    def pass_y(slots, group=None):
-        return start(
-            texts.at[0, rest, rest, :, tail],
+            passed,
+        )
+
+    def pass_y(slots):
+        start(
+            texts.at[0, rest],
             [(texts.at[0, slots, 0, :, tail], texts.at[0, slots, SLOT[4 - k], :, tail], along_y(k)) for k in steps],
-            group,
+            passed,
         )
 
     arrived(from_block)
     block = pl.ds(ROWS, 3 * ROWS)
-    from_x = start(
-        images.at[pl.ds(0, 9 * ROWS)],
+    start(
+        images.at[block],
         [
             (images.at[block], images.at[pl.ds((4 - k) * bundle + ROWS, 3 * ROWS)], along_x(k))
             for k in steps
         ],
+        from_x,
     )
     arrived(head_y)
-    passed_z = pass_z(near)
+    pass_z(near)
     arrived(tail_z)
-    passed_y = pass_y(near)
+    pass_y(near)
     arrived(head_y_far)
-    pass_z(far, passed_z)
+    pass_z(far)
     arrived(tail_z_far)
-    pass_y(far, passed_y)
+    pass_y(far)
     for made in loads:
         made.wait()
     scaling = numbers[0, 0]
     offset = numbers[1, 0]
-    arrived(own_x, from_x)
+    arrived(from_x)
     image_share = start(
         images.at[pl.ds(SET, SET)], [(images.at[pl.ds(0, SET)], images.at[pl.ds(SET, SET)], sibling)]
     )
-    arrived(tail_y, head_z, passed_z, passed_y)
+    arrived(passed)
     text_share = start(texts.at[1], [(texts.at[0], texts.at[1], sibling)])
 
     rows = lax.broadcasted_iota(jnp.int32, (SET, SET), 0)
@@ -344,9 +348,10 @@
             for k in range(3):
                 total = total + came_z[k, at - 1].astype(F32)
             text_parts[0, at, :, 0:CUT] = total.astype(BF16)
-        return start(
-            last_y.at[pl.ds(slots[0] - 1, len(slots)), :, head],
-            [(text_parts.at[0, SLOT[k], :, head], last_y.at[SLOT[4 - k] - 1, :, head], along_y(k)) for k in ways],
+        start(
+            last_text,
+            [(text_parts.at[0, SLOT[k], :, head], last_text.at[0, SLOT[4 - k] - 1, :, head], along_y(k)) for k in ways],
+            text_end,
         )
 
     def out_z(slots, ways):
@@ -355,58 +360,60 @@
             for k in range(3):
                 total = total + came_y[k, at - 1].astype(F32)
             text_parts[at, 0, :, CUT:] = total.astype(BF16)
-        return start(
-            last_z.at[pl.ds(slots[0] - 1, len(slots)), :, tail],
-            [(text_parts.at[SLOT[k], 0, :, tail], last_z.at[SLOT[4 - k] - 1, :, tail], along_z(k)) for k in ways],
-        )
-
+        start(
+            last_text,
+            [(text_parts.at[SLOT[k], 0, :, tail], last_text.at[1, SLOT[4 - k] - 1, :, tail], along_z(k)) for k in ways],
+            text_end,
+        )
+
+    text_end = start(last_text, [])
+    image_end = start(last_image, [])
     arrived(to_z_far)
-    outs = [out_y((3,), (2,))]
+    out_y((3,), (2,))
     arrived(to_y_far)
-    outs.append(out_z((3,), (2,)))
-    last_x = start(
-        came_last,
-        [(image_parts.at[pl.ds((k - 1) * bundle, ROWS)], came_last.at[3 - k], along_x(k)) for k in steps],
-    )
-    direct_y = start(
-        last_y.at[:, :, tail],
-        [(text_parts.at[0, SLOT[k], :, tail], last_y.at[SLOT[4 - k] - 1, :, tail], along_y(k)) for k in steps],
-    )
-    direct_z = start(
-        last_z.at[:, :, head],
-        [(text_parts.at[SLOT[k], 0, :, head], last_z.at[SLOT[4 - k] - 1, :, head], along_z(k)) for k in steps],
+    out_z((3,), (2,))
+    start(
+        last_image,
+        [(image_parts.at[pl.ds((k - 1) * bundle, ROWS)], last_image.at[0, 3 - k], along_x(k)) for k in steps],
+        image_end,
+    )
+    start(
+        last_text,
+        [(text_parts.at[0, SLOT[k], :, tail], last_text.at[0, SLOT[4 - k] - 1, :, tail], along_y(k)) for k in steps]
+        + [(text_parts.at[SLOT[k], 0, :, head], last_text.at[1, SLOT[4 - k] - 1, :, head], along_z(k)) for k in steps],
+        text_end,
     )
     arrived(to_z_near)
-    outs.append(out_y((1, 2), (1, 3)))
+    out_y((1, 2), (1, 3))
     arrived(to_y_near)
-    outs.append(out_z((1, 2), (1, 3)))
+    out_z((1, 2), (1, 3))
     arrived(to_x)
     total = image_own[ROWS:]
     for k in range(3):
         total = total + came_x[k].astype(F32)
     block_parts[...] = total.astype(BF16)
-    out_block = start(
-        last_block,
+    start(
+        last_image,
         [
-            (block_parts.at[pl.ds((k - 1) * ROWS, ROWS)], last_block.at[k - 1], in_block(k))
+            (block_parts.at[pl.ds((k - 1) * ROWS, ROWS)], last_image.at[1, k - 1], in_block(k))
             for k in (3, 1, 2)
         ],
+        image_end,
     )
     on_core_1(lambda: give(2, take(1)))
-    arrived(direct_y, direct_z, *outs)
+    arrived(text_end)
     total = text_own[...]
     for k in range(3):
-        total = total + last_y[k].astype(F32) + last_z[k].astype(F32)
+        total = total + last_text[0, k].astype(F32) + last_text[1, k].astype(F32)
     text_grad_ref[...] = total
-    arrived(last_x, out_block)
+    arrived(image_end)
     total = image_own[0:ROWS]
     for k in range(3):
-        total = total + came_last[k].astype(F32) + last_block[k].astype(F32)
+        total = total + last_image[0, k].astype(F32) + last_image[1, k].astype(F32)
     image_grad_ref[...] = total
     on_core_1(loss_end)
     on_core_0(loss_got)
-    for group, whole in enumerate(groups):
-        pltpu.make_async_copy(whole, whole, send.at[group]).wait()
+    pltpu.make_async_copy(all_sent, all_sent, send).wait()
 
 
 def finish(loss_ref, image_ref, text_ref, loss_out, image_out, text_out, sems):
@@ -443,19 +450,18 @@
             pltpu.VMEM((ROWS, width), F32),
             pltpu.VMEM((3, 3, ROWS, CUT), BF16),
             pltpu.VMEM((3, 3, ROWS, width - CUT), BF16),
-            pltpu.VMEM((3, ROWS, width), BF16),
-            pltpu.VMEM((3, ROWS, width), BF16),
+            pltpu.VMEM((2, 3, ROWS, width), BF16),
             pltpu.VMEM((12 * ROWS, width), BF16),
             pltpu.VMEM((4 * ROWS, width), F32),
             pltpu.VMEM((3, 3 * ROWS, width), BF16),
-            pltpu.VMEM((3, ROWS, width), BF16),
             pltpu.VMEM((3 * ROWS, width), BF16),
-            pltpu.VMEM((3, ROWS, width), BF16),
+            pltpu.VMEM((2, 3, ROWS, width), BF16),
             pltpu.VMEM((3, 8, 8, 128), F32),
+            pltpu.VMEM((SENT, width), BF16),
             pltpu.SMEM((2, 1), F32),
             dma((4,)),
-            dma((26,)),
-            dma((26,)),
+            dma,
+            dma((GROUPS,)),
             pltpu.VMEM((4, 8, 128), F32),
             dma((4,)),
             dma((3,)),

time: 47.4 us -> 47 us (level)
  no operation moved by 1% of the time
where the time goes in v6:
time: 47 us; the launch traced here: 46.7 us
  Pallas kernels  44.8 us (95%)
  between operations  1.93 us (4%)
    pallas_call x1, Pallas kernels, local(): pl.pallas_call(kernel, out_shape=(jax.ShapeDtypeStruct((8, 128), F32), gr...  44.1 us

profile of v6, /device:TPU:1, one launch (start us, length us, event | category | flops | bytes accessed | tf_op | source)
XLA Modules:
  0.0 46.7 jit_solution(17095857031596924044)
XLA Ops:
  1.9 44.1 %pairs.1 = (f32[8,128]{1,0:T(8,128)S(1)}, f32[16,1152]{1,0:T(8,128)S(1)}, f32[16,1152]{1,0:T(8,128)S(1)}) custom-call(bf16[16,1152]{1,0:T(8,128)(2,1)} %image_ref.1, bf16[16,1152]{1,0:T(8,128)(2,1)} %text_ref.1, f32[1]{0:T(128)S(6)} %copy.7.scale_ref, f32[1]{0:T(128)S(6)} %copy.8.bias_ref), custom_call_target="tpu_custom_call" | custom-call | tf_op jit(solution)/shard_map/pairs/pallas_call | solution.py:437
  46.0 0.7 %finish.1 = (f32[1,128]{1,0:T(1,128)}, f32[16,1152]{1,0:T(8,128)}, f32[16,1152]{1,0:T(8,128)}) custom-call(f32[8,128]{1,0:T(8,128)S(1)} %get-tuple-element.9.loss_ref, f32[16,1152]{1,0:T(8,128)S(1)} %get-tuple-element.10.image_ref, f32[16,1152]{1,0:T(8,128)S(1)} %get-tuple-element.11.text_ref), custom_call_target="tpu_custom_call" | custom-call | tf_op jit(solution)/shard_map/finish/pallas_call | solution.py:480

commit v7 on v6

--- a/solution.py
+++ b/solution.py
@@ -292,9 +292,8 @@
     def text_set(half):
         return texts[half].reshape(SET, width)
 
+    arrived(image_share)
     for half in (0, 1):
-        if half == 1:
-            arrived(image_share)
         part = slice(half * SET, (half + 1) * SET)
         mask = diagonal if half == 0 else None
         dots = lax.dot_general(text_set(0), images[part], NT, preferred_element_type=F32)

time: 47 us -> 47.2 us (level)
  no operation moved by 1% of the time
where the time goes in v7:
time: 47.2 us; the launch traced here: 47.1 us
  Pallas kernels  45.2 us (96%)
  between operations  1.93 us (4%)
    pallas_call x1, Pallas kernels, local(): pl.pallas_call(kernel, out_shape=(jax.ShapeDtypeStruct((8, 128), F32), gr...  44.5 us

profile of v7, /device:TPU:1, one launch (start us, length us, event | category | flops | bytes accessed | tf_op | source)
XLA Modules:
  0.0 47.1 jit_solution(5576346143033585278)
XLA Ops:
  1.9 44.5 %pairs.1 = (f32[8,128]{1,0:T(8,128)S(1)}, f32[16,1152]{1,0:T(8,128)S(1)}, f32[16,1152]{1,0:T(8,128)S(1)}) custom-call(bf16[16,1152]{1,0:T(8,128)(2,1)} %image_ref.1, bf16[16,1152]{1,0:T(8,128)(2,1)} %text_ref.1, f32[1]{0:T(128)S(6)} %copy.7.scale_ref, f32[1]{0:T(128)S(6)} %copy.8.bias_ref), custom_call_target="tpu_custom_call" | custom-call | tf_op jit(solution)/shard_map/pairs/pallas_call | solution.py:436
  46.4 0.7 %finish.1 = (f32[1,128]{1,0:T(1,128)}, f32[16,1152]{1,0:T(8,128)}, f32[16,1152]{1,0:T(8,128)}) custom-call(f32[8,128]{1,0:T(8,128)S(1)} %get-tuple-element.9.loss_ref, f32[16,1152]{1,0:T(8,128)S(1)} %get-tuple-element.10.image_ref, f32[16,1152]{1,0:T(8,128)S(1)} %get-tuple-element.11.text_ref), custom_call_target="tpu_custom_call" | custom-call | tf_op jit(solution)/shard_map/finish/pallas_call | solution.py:479

commit v8 on v7

--- a/solution.py
+++ b/solution.py
@@ -110,11 +110,10 @@
     sibling = device(x, y, z, 1 - core)
 
     barrier = pltpu.get_barrier_semaphore()
-    for reach in (ring_y, ring_z):
-        for k in all_steps:
+    for reach in (along_y, along_z, along_x, in_block):
+        for k in steps:
             pl.semaphore_signal(barrier, inc=1, device_id=reach(k), device_id_type=MESH)
-    for to in (along_x(2), along_x(1), along_x(3), in_block(3), sibling):
-        pl.semaphore_signal(barrier, inc=1, device_id=to, device_id_type=MESH)
+    pl.semaphore_signal(barrier, inc=1, device_id=sibling, device_id_type=MESH)
     loads = [
         pltpu.make_async_copy(image_ref, images.at[pl.ds(0, ROWS)], load.at[0]),
         pltpu.make_async_copy(text_ref, texts.at[0, 0, 0], load.at[1]),
@@ -123,7 +122,7 @@
     ]
     for made in loads:
         made.start()
-    pl.semaphore_wait(barrier, 19)
+    pl.semaphore_wait(barrier, 13)
 
     groups = []
 

time: 47.2 us -> 46.8 us (level)
  no operation moved by 1% of the time
where the time goes in v8:
time: 46.8 us; the launch traced here: 46.7 us
  Pallas kernels  44.8 us (96%)
  between operations  1.93 us (4%)
    pallas_call x1, Pallas kernels, local(): pl.pallas_call(kernel, out_shape=(jax.ShapeDtypeStruct((8, 128), F32), gr...  44.1 us

profile of v8, /device:TPU:1, one launch (start us, length us, event | category | flops | bytes accessed | tf_op | source)
XLA Modules:
  0.0 46.7 jit_solution(14866109196126540432)
XLA Ops:
  1.9 44.1 %pairs.1 = (f32[8,128]{1,0:T(8,128)S(1)}, f32[16,1152]{1,0:T(8,128)S(1)}, f32[16,1152]{1,0:T(8,128)S(1)}) custom-call(bf16[16,1152]{1,0:T(8,128)(2,1)} %image_ref.1, bf16[16,1152]{1,0:T(8,128)(2,1)} %text_ref.1, f32[1]{0:T(128)S(6)} %copy.7.scale_ref, f32[1]{0:T(128)S(6)} %copy.8.bias_ref), custom_call_target="tpu_custom_call" | custom-call | tf_op jit(solution)/shard_map/pairs/pallas_call | solution.py:435
  46.0 0.7 %finish.1 = (f32[1,128]{1,0:T(1,128)}, f32[16,1152]{1,0:T(8,128)}, f32[16,1152]{1,0:T(8,128)}) custom-call(f32[8,128]{1,0:T(8,128)S(1)} %get-tuple-element.9.loss_ref, f32[16,1152]{1,0:T(8,128)S(1)} %get-tuple-element.10.image_ref, f32[16,1152]{1,0:T(8,128)S(1)} %get-tuple-element.11.text_ref), custom_call_target="tpu_custom_call" | custom-call | tf_op jit(solution)/shard_map/finish/pallas_call | solution.py:478

commit v9 on v8

--- a/solution.py
+++ b/solution.py
@@ -87,7 +87,6 @@
     steps = (2, 1, 3)
     flipped_y = y + 1 - 2 * lax.rem(y, 2)
     flipped_z = z + 1 - 2 * lax.rem(z, 2)
-    all_steps = (4, 3, 5, 2, 6, 1, 7)
 
     def along_x(k):
         return device(lax.rem(x + k, 4), y, z, core)
@@ -225,7 +224,22 @@
     columns = lax.broadcasted_iota(jnp.int32, (SET, SET), 1)
     diagonal = (rows == columns) & (rows < ROWS)
 
-    stages = ((y, ring_y, all_steps), (z, ring_z, all_steps), (x, along_x, steps))
+    def in_plane(k):
+        return device(lax.rem(x + k % 4, 4), lax.rem(y + 2 * (k // 4), 8), z, core)
+
+    def in_column(k):
+        return device(x, flipped_y if k % 2 else y, lax.rem(z + k // 2, 8), core)
+
+    def plane_hops(k):
+        return (0, 1, 2, 1)[k % 4] + (0, 2, 4, 2)[k // 4]
+
+    def column_hops(k):
+        return k % 2 + min(k // 2, 8 - k // 2)
+
+    stages = (
+        (4 * x + lax.div(y, 2), in_plane, sorted(range(1, 16), key=plane_hops, reverse=True)),
+        (2 * z + lax.rem(y, 2), in_column, sorted(range(1, 16), key=column_hops, reverse=True)),
+    )
 
     def across(src, dst, at):
         return pltpu.make_async_remote_copy(
@@ -275,11 +289,13 @@
         give(0, shared_loss[0] + shared_loss[1])
 
     def loss_end():
-        shared_loss[2] = take(2)
+        shared_loss[2] = take(1)
         across(shared_loss.at[2], shared_loss.at[3], 2).start()
         loss_ref[...] = jnp.full(loss_ref.shape, jnp.sum(shared_loss[2]) / 8192.0, F32)
+
+    def loss_sent():
         across(shared_loss.at[2], shared_loss.at[3], 2).wait_send()
-        for stage in range(3):
+        for stage in range(2):
             whole = ring(stage)[1]
             pltpu.make_async_copy(whole, whole, loss_send.at[stage]).wait()
 
@@ -339,7 +355,6 @@
             for k in steps
         ],
     )
-    on_core_1(lambda: give(1, take(0)))
     def out_y(slots, ways):
         for at in slots:
             total = text_near[at - 1]
@@ -385,6 +400,7 @@
     out_y((1, 2), (1, 3))
     arrived(to_y_near)
     out_z((1, 2), (1, 3))
+    on_core_1(lambda: give(1, take(0)))
     arrived(to_x)
     total = image_own[ROWS:]
     for k in range(3):
@@ -398,18 +414,18 @@
         ],
         image_end,
     )
-    on_core_1(lambda: give(2, take(1)))
     arrived(text_end)
     total = text_own[...]
     for k in range(3):
         total = total + last_text[0, k].astype(F32) + last_text[1, k].astype(F32)
     text_grad_ref[...] = total
+    on_core_1(loss_end)
     arrived(image_end)
     total = image_own[0:ROWS]
     for k in range(3):
         total = total + last_image[0, k].astype(F32) + last_image[1, k].astype(F32)
     image_grad_ref[...] = total
-    on_core_1(loss_end)
+    on_core_1(loss_sent)
     on_core_0(loss_got)
     pltpu.make_async_copy(all_sent, all_sent, send).wait()
 
@@ -454,7 +470,7 @@
             pltpu.VMEM((3, 3 * ROWS, width), BF16),
             pltpu.VMEM((3 * ROWS, width), BF16),
             pltpu.VMEM((2, 3, ROWS, width), BF16),
-            pltpu.VMEM((3, 8, 8, 128), F32),
+            pltpu.VMEM((2, 16, 8, 128), F32),
             pltpu.VMEM((SENT, width), BF16),
             pltpu.SMEM((2, 1), F32),
             dma((4,)),
@@ -462,8 +478,8 @@
             dma((GROUPS,)),
             pltpu.VMEM((4, 8, 128), F32),
             dma((4,)),
-            dma((3,)),
-            dma((3,)),
+            dma((2,)),
+            dma((2,)),
         ],
         compiler_params=pltpu.CompilerParams(
             collective_id=0, has_side_effects=True, vmem_limit_bytes=48 * 2**20

time: 46.8 us -> 45.8 us (0.979)
  Pallas kernels: 44.8 us -> 43.8 us
    pallas_call x1, Pallas kernels: 44.1 us -> 43.1 us  [local(): pl.pallas_call(kernel, out_shape=(jax.ShapeDtypeStruct((8, 128), F32), gr...]
where the time goes in v9:
time: 45.8 us; the launch traced here: 45.7 us
  Pallas kernels  43.8 us (96%)
  between operations  1.93 us (4%)
    pallas_call x1, Pallas kernels, local(): pl.pallas_call(kernel, out_shape=(jax.ShapeDtypeStruct((8, 128), F32), gr...  43.1 us

profile of v9, /device:TPU:1, one launch (start us, length us, event | category | flops | bytes accessed | tf_op | source)
XLA Modules:
  0.0 45.7 jit_solution(5706365787645338559)
XLA Ops:
  1.9 43.1 %pairs.1 = (f32[8,128]{1,0:T(8,128)S(1)}, f32[16,1152]{1,0:T(8,128)S(1)}, f32[16,1152]{1,0:T(8,128)S(1)}) custom-call(bf16[16,1152]{1,0:T(8,128)(2,1)} %image_ref.1, bf16[16,1152]{1,0:T(8,128)(2,1)} %text_ref.1, f32[1]{0:T(128)S(6)} %copy.7.scale_ref, f32[1]{0:T(128)S(6)} %copy.8.bias_ref), custom_call_target="tpu_custom_call" | custom-call | tf_op jit(solution)/shard_map/pairs/pallas_call | solution.py:451
  45.0 0.7 %finish.1 = (f32[1,128]{1,0:T(1,128)}, f32[16,1152]{1,0:T(8,128)}, f32[16,1152]{1,0:T(8,128)}) custom-call(f32[8,128]{1,0:T(8,128)S(1)} %get-tuple-element.9.loss_ref, f32[16,1152]{1,0:T(8,128)S(1)} %get-tuple-element.10.image_ref, f32[16,1152]{1,0:T(8,128)S(1)} %get-tuple-element.11.text_ref), custom_call_target="tpu_custom_call" | custom-call | tf_op jit(solution)/shard_map/finish/pallas_call | solution.py:494

commit v10 on v9

--- a/solution.py
+++ b/solution.py
@@ -398,9 +398,9 @@
     )
     arrived(to_z_near)
     out_y((1, 2), (1, 3))
+    on_core_1(lambda: give(1, take(0)))
     arrived(to_y_near)
     out_z((1, 2), (1, 3))
-    on_core_1(lambda: give(1, take(0)))
     arrived(to_x)
     total = image_own[ROWS:]
     for k in range(3):
@@ -414,12 +414,12 @@
         ],
         image_end,
     )
+    on_core_1(loss_end)
     arrived(text_end)
     total = text_own[...]
     for k in range(3):
         total = total + last_text[0, k].astype(F32) + last_text[1, k].astype(F32)
     text_grad_ref[...] = total
-    on_core_1(loss_end)
     arrived(image_end)
     total = image_own[0:ROWS]
     for k in range(3):

time: 45.8 us -> 45.9 us (level)
  no operation moved by 1% of the time
where the time goes in v10:
time: 45.9 us; the launch traced here: 45.7 us
  Pallas kernels  43.8 us (95%)
  between operations  1.93 us (4%)
    pallas_call x1, Pallas kernels, local(): pl.pallas_call(kernel, out_shape=(jax.ShapeDtypeStruct((8, 128), F32), gr...  43.1 us

profile of v10, /device:TPU:1, one launch (start us, length us, event | category | flops | bytes accessed | tf_op | source)
XLA Modules:
  0.0 45.7 jit_solution(15865891041465549696)
XLA Ops:
  1.9 43.1 %pairs.1 = (f32[8,128]{1,0:T(8,128)S(1)}, f32[16,1152]{1,0:T(8,128)S(1)}, f32[16,1152]{1,0:T(8,128)S(1)}) custom-call(bf16[16,1152]{1,0:T(8,128)(2,1)} %image_ref.1, bf16[16,1152]{1,0:T(8,128)(2,1)} %text_ref.1, f32[1]{0:T(128)S(6)} %copy.7.scale_ref, f32[1]{0:T(128)S(6)} %copy.8.bias_ref), custom_call_target="tpu_custom_call" | custom-call | tf_op jit(solution)/shard_map/pairs/pallas_call | solution.py:451
  45.0 0.7 %finish.1 = (f32[1,128]{1,0:T(1,128)}, f32[16,1152]{1,0:T(8,128)}, f32[16,1152]{1,0:T(8,128)}) custom-call(f32[8,128]{1,0:T(8,128)S(1)} %get-tuple-element.9.loss_ref, f32[16,1152]{1,0:T(8,128)S(1)} %get-tuple-element.10.image_ref, f32[16,1152]{1,0:T(8,128)S(1)} %get-tuple-element.11.text_ref), custom_call_target="tpu_custom_call" | custom-call | tf_op jit(solution)/shard_map/finish/pallas_call | solution.py:494
